TPU v7x, 32 devices: a whole 2x2x4 slice. The times are simulated.
32 devices in a mesh: ctx: 4 (over x, core), tp: 8 (over z, y).
Axes of the slice: x: 2, y: 2, z: 4, core: 2. Of those that a mesh axis runs over, the one named last changes fastest.
Arguments:
- queries: bfloat16 [512, 3072], P('ctx', 'tp'), may hold values from -80 to 80
- key_rows: bfloat16 [512, 512], P('ctx'), may hold values from -4 to 4
- value_rows: bfloat16 [512, 512], P('ctx'), may hold values from -6 to 6
- out_grad: bfloat16 [512, 3072], P('ctx', 'tp'), may hold values from -6 to 6
- attn_out: bfloat16 [512, 3072], P('ctx', 'tp'), may hold values from -6 to 6
- doc_ids: int32 [512], replicated, may hold values from 0 to 7, never falling along the last dimension, each value on 1 to 384 neighbouring positions
- row_grad: bfloat16 [512, 6144], P('ctx', 'tp'), may hold values from -6 to 6
- gate_weights: float32 [512, 2], P('ctx'), may hold values from 0.1 to 0.9
- expert_ids: int32 [512, 2], P('ctx'), may hold values from 0 to 3, all different within a row; in each aligned block of 128 rows (0 to 127, 128 to 255, ...) at most 128 rows name the same one
- expert_out: bfloat16 [4, 512, 6144], P('ctx', 'tp'), may hold values from -0.079589844 to 0.079589844
Outputs:
- query_grad: bfloat16 [512, 3072], P('ctx', 'tp')
- key_grad: bfloat16 [512, 512], P('ctx', 'tp')
- value_grad: bfloat16 [512, 512], P('ctx', 'tp')
- gate_grad: float32 [4, 512], P('ctx', 'tp')
- expert_grad: bfloat16 [4, 512, 6144], P('ctx', 'tp')
Inputs may be any that keep to these rules, and one draw needn't show every extreme that they name: `doc_ids`: never falling along the tokens; each document holds 1 to 384 tokens and one holds exactly 384. `expert_ids`: A token's 2 experts differ; within each aligned block of 128 tokens no expert is named by more than 128 entries, and in some block an expert is named by exactly 128.
All inputs are finite; a program needn't handle non-finite values.
Results may differ from a plain program's by a relative error of at most 0.006.
Values may be sent and summed in bfloat16 or wider, within the bound.
A program may use at most 64 MiB of HBM per device.

v0:
```python
import math

import jax
import jax.numpy as jnp
from jax import lax
from jax.sharding import PartitionSpec as P

HD = 128
QH_DEV = 3
TOP = 2


def shifted(x, axis, by):
    size = lax.axis_size(axis)
    pairs = [(i, i + by) for i in range(size) if 0 <= i + by < size]
    return lax.ppermute(x, axis, pairs)


def from_partner(value, axis, distance):
    mask = 2**distance
    pairs = [(source, source ^ mask) for source in range(lax.axis_size(axis))]
    return lax.ppermute(value, axis, pairs)


def slot_table(routes_block, experts_total, capacity):
    flat_ids = routes_block.reshape(-1)
    onehot = (flat_ids[:, None] == jnp.arange(experts_total, dtype=jnp.int32)[None, :]).astype(
        jnp.int32
    )
    earlier = jnp.cumsum(onehot, axis=0) - onehot
    ranking = jnp.sum(earlier * onehot, axis=1)
    return (2 * flat_ids + ranking // capacity) * capacity + ranking % capacity


def split_halves(terms, half_index):
    quarter = HD // 2
    other_index = 1 - half_index
    keep_part = jnp.concatenate(
        [
            lax.dynamic_slice_in_dim(terms, half_index * quarter, quarter, 1),
            lax.dynamic_slice_in_dim(terms, HD + half_index * quarter, quarter, 1),
        ],
        axis=1,
    )
    send_part = jnp.concatenate(
        [
            lax.dynamic_slice_in_dim(terms, other_index * quarter, quarter, 1),
            lax.dynamic_slice_in_dim(terms, HD + other_index * quarter, quarter, 1),
        ],
        axis=1,
    )
    return (keep_part, send_part)


def local(
    queries,
    key_rows,
    value_rows,
    out_grad,
    attn_out,
    doc_ids,
    row_grad,
    gate_weights,
    expert_ids,
    expert_out,
):
    tensor_index = lax.axis_index("tp")
    context_index = lax.axis_index("ctx")
    local_rows = queries.shape[0]
    scaling = 1.0 / math.sqrt(HD)
    group_index = tensor_index // 2
    own_keys = lax.dynamic_slice_in_dim(key_rows, group_index * HD, HD, 1)
    own_values = lax.dynamic_slice_in_dim(value_rows, group_index * HD, HD, 1)
    all_keys, all_values = (
        lax.all_gather(own_keys, "ctx", axis=0, tiled=True),
        lax.all_gather(own_values, "ctx", axis=0, tiled=True),
    )
    total_rows = all_keys.shape[0]
    longest = total_rows // 2 + local_rows
    window = longest + local_rows
    window_start = jnp.maximum((context_index + 1) * local_rows - window, 0)
    window_keys = lax.dynamic_slice_in_dim(all_keys, window_start, window, 0)
    window_values = lax.dynamic_slice_in_dim(all_values, window_start, window, 0)
    window_docs = lax.dynamic_slice_in_dim(doc_ids, window_start, window, 0)
    query_pos = context_index * local_rows + jnp.arange(local_rows, dtype=jnp.int32)
    key_pos = window_start + jnp.arange(window, dtype=jnp.int32)
    query_docs = lax.dynamic_slice_in_dim(doc_ids, context_index * local_rows, local_rows, 0)
    allowed = (query_docs[:, None] == window_docs[None, :]) & (
        key_pos[None, :] <= query_pos[:, None]
    )
    query_parts = []
    score_list = []
    prob_list = []
    query_list = []
    grad_list = []
    for head_slot in range(QH_DEV):
        query_head = queries[:, head_slot * HD : (head_slot + 1) * HD]
        grad_head = out_grad[:, head_slot * HD : (head_slot + 1) * HD]
        output_head = attn_out[:, head_slot * HD : (head_slot + 1) * HD]
        scores = jnp.dot(query_head, window_keys.T, preferred_element_type=jnp.float32) * scaling
        scores = jnp.where(allowed, scores, -1e30)
        row_max = jnp.max(scores, axis=1, keepdims=True)
        totals = jnp.sum(jnp.where(allowed, jnp.exp(scores - row_max), 0.0), axis=1, keepdims=True)
        log_total = row_max + jnp.log(totals)
        probs = jnp.where(allowed, jnp.exp(scores - log_total), 0.0)
        row_delta = jnp.sum(
            grad_head.astype(jnp.float32) * output_head.astype(jnp.float32), axis=1, keepdims=True
        )
        prob_grad = jnp.dot(grad_head, window_values.T, preferred_element_type=jnp.float32)
        score_grad = (probs * (prob_grad - row_delta)).astype(jnp.bfloat16)
        query_parts.append(
            (jnp.dot(score_grad, window_keys, preferred_element_type=jnp.float32) * scaling).astype(
                jnp.bfloat16
            )
        )
        score_list.append(score_grad)
        prob_list.append(probs.astype(jnp.bfloat16))
        query_list.append(query_head)
        grad_list.append(grad_head)
    query_grad = jnp.concatenate(query_parts, axis=1)
    stacked_scores = jnp.stack(score_list)
    stacked_probs = jnp.stack(prob_list)
    stacked_queries = jnp.stack(query_list)
    stacked_grads = jnp.stack(grad_list)

    def window_terms(start, count):
        score_block = lax.dynamic_slice_in_dim(stacked_scores, start, count, 2)
        prob_block = lax.dynamic_slice_in_dim(stacked_probs, start, count, 2)
        key_part = (
            jnp.einsum(
                "hqk,hqd->kd", score_block, stacked_queries, preferred_element_type=jnp.float32
            )
            * scaling
        )
        value_part = jnp.einsum(
            "hqk,hqd->kd", prob_block, stacked_grads, preferred_element_type=jnp.float32
        )
        return jnp.concatenate([key_part, value_part], axis=1)

    half_index = tensor_index % 2
    reach = longest // local_rows

    def window_term(offset):
        target = context_index - offset
        local_start = jnp.clip(target * local_rows - window_start, 0, window - local_rows)
        valid = (target >= 0).astype(jnp.float32)
        return window_terms(local_start, local_rows) * valid

    def window_step(step_index, running):
        running = shifted(running, "ctx", -1)
        return running + window_term(reach - step_index)

    summed = lax.fori_loop(1, reach + 1, window_step, window_term(reach))
    keep_part, send_part = split_halves(summed, half_index)
    partner = from_partner(send_part, "tp", 0)
    combined = keep_part + partner
    key_grad = combined[:, : HD // 2].astype(jnp.bfloat16)
    value_grad = combined[:, HD // 2 :].astype(jnp.bfloat16)
    group_slots = expert_out.shape[1]
    tensor_count = lax.axis_size("tp")
    slot_count = tensor_count * group_slots
    positions = slot_table(expert_ids, tensor_count // 2, group_slots)
    chosen = (jnp.arange(slot_count, dtype=jnp.int32)[:, None] == positions[None, :]).astype(
        jnp.int32
    )
    by_token = jnp.sum(chosen.reshape(slot_count, local_rows, TOP), axis=2)
    full_rows = lax.all_gather(row_grad, "tp", axis=1, tiled=True)
    my_tokens = lax.dynamic_slice_in_dim(by_token, tensor_index * group_slots, group_slots, 0)
    arrived = jnp.dot(
        my_tokens.astype(jnp.bfloat16), full_rows, preferred_element_type=jnp.float32
    ).astype(jnp.bfloat16)
    my_entries = lax.dynamic_slice_in_dim(chosen, tensor_index * group_slots, group_slots, 0)
    slot_gates = jnp.sum(jnp.where(my_entries > 0, gate_weights.reshape(-1)[None, :], 0.0), axis=1)
    arrived_wide = arrived.astype(jnp.float32)
    gate_grad = jnp.sum(arrived_wide * expert_out[0].astype(jnp.float32), axis=1)[None, :]
    expert_grad = (slot_gates[:, None] * arrived_wide).astype(jnp.bfloat16)[None]
    return (query_grad, key_grad, value_grad, gate_grad, expert_grad)


def solution(mesh):
    in_specs = (
        P("ctx", "tp"),
        P("ctx", None),
        P("ctx", None),
        P("ctx", "tp"),
        P("ctx", "tp"),
        P(),
        P("ctx", "tp"),
        P("ctx", None),
        P("ctx", None),
        P("ctx", "tp", None),
    )
    out_specs = (
        P("ctx", "tp"),
        P("ctx", "tp"),
        P("ctx", "tp"),
        P("ctx", "tp"),
        P("ctx", "tp", None),
    )
    return jax.shard_map(local, mesh=mesh, in_specs=in_specs, out_specs=out_specs, check_vma=False)
```

profile of v0, /device:TPU:0, one launch (start us, length us, event | category | flops | bytes accessed | tf_op | source)
XLA Modules:
  0.0 68.3 jit_solution(7382332696472477065)
XLA Ops:
  7.2 0.0 copy-start
  7.2 0.0 copy-start.5
  7.2 0.0 all-gather.2.cloned.1.call-start
  7.2 0.7 all-gather.2.cloned.1.call-update
  8.0 0.1 copy-done
  8.1 6.6 %all_gather.9 = bf16[512,128]{1,0:T(8,128)(2,1)S(1)} all-gather(bf16[128,128]{1,0:T(8,128)(2,1)S(1)} %constant_dynamic-slice_fusion.5), channel_id=1, replica_groups=mesh['ctx'=4,'tp'=8] {'ctx'}, dimensions={0}, use_global_device_ids=true | all-gather | bytes 163840 | tf_op jit(solution)/shard_map/all_gather | solution.py:75
  14.7 0.8 %dynamic_slice.50 = s32[128]{0:T(128)S(1)} dynamic-slice(s32[512]{0:T(512)} %param.17, s32[]{:T(128)S(6)} %select_n.100), dynamic_slice_sizes={128} | dynamic-slice | bytes 1028 | tf_op jit(solution)/shard_map/dynamic_slice | solution.py:87
  15.5 1.0 %fusion.57 = (f32[128]{0:T(128)S(1)}, f32[128,512]{0,1:T(8,128)S(1)}) fusion(bf16[512,128]{1,0:T(8,128)(2,1)S(1)} %all_gather.9, bf16[128,384]{1,0:T(8,128)(2,1)} %param.12, s32[128]{0:T(128)S(1)} %iota_add_fusion.1, s32[512]{0:T(512)S(1)} %iota_add_fusion, s32[512]{0:T(512)} %param.17, s32[128]{0:T(128)S(1)} %dynamic_slice.50), kind=kOutput, calls=%fused_computation.123 | convolution fusion | flops 17170304 | bytes 431616 | tf_op jit(solution)/shard_map/dot_general | solution.py:100
  16.5 1.0 %fusion.58 = (f32[128]{0:T(128)S(1)}, f32[128,512]{0,1:T(8,128)S(1)}) fusion(bf16[512,128]{1,0:T(8,128)(2,1)S(1)} %all_gather.9, bf16[128,384]{1,0:T(8,128)(2,1)} %param.12, s32[128]{0:T(128)S(1)} %iota_add_fusion.1, s32[512]{0:T(512)S(1)} %iota_add_fusion, s32[512]{0:T(512)} %param.17, s32[128]{0:T(128)S(1)} %dynamic_slice.50), kind=kOutput, calls=%fused_computation.124 | convolution fusion | flops 17170304 | bytes 431616 | tf_op jit(solution)/shard_map/dot_general | solution.py:100
  17.5 0.2 fusion.59
  17.8 0.2 select_reduce_fusion.2
  18.0 0.8 %constant_dynamic-slice_fusion.4 = bf16[128,128]{1,0:T(8,128)(2,1)S(1)} fusion(bf16[128,512]{1,0:T(8,128)(2,1)} %param.14, s32[]{:T(128)S(6)} %select_n.102), kind=kLoop, calls=%fused_computation.92 | loop fusion | bytes 65540 | tf_op jit(solution)/shard_map/dynamic_slice | solution.py:73
  18.8 5.6 %all_gather.10 = bf16[512,128]{1,0:T(8,128)(2,1)S(1)} all-gather(bf16[128,128]{1,0:T(8,128)(2,1)S(1)} %constant_dynamic-slice_fusion.4), channel_id=1, replica_groups=mesh['ctx'=4,'tp'=8] {'ctx'}, dimensions={0}, use_global_device_ids=true | all-gather | bytes 163840 | tf_op jit(solution)/shard_map/all_gather | solution.py:76
  24.4 0.1 copy.107
  24.6 0.1 copy.108
  24.7 0.1 copy.110
  24.8 0.1 copy.111
  24.9 0.1 copy.113
  25.0 0.1 copy.114
  25.3 0.2 fusion.20
  25.5 0.2 fusion.21
  25.7 0.2 fusion.33
  26.0 0.2 fusion.22
  26.2 0.1 copy.106
  26.3 0.1 copy.109
  26.5 0.1 copy.112
  26.6 0.1 pad_maximum_fusion
  26.7 0.2 fusion.23
  26.9 0.2 convolution_bitcast_fusion.2
  27.2 16.2 %while.13 = (s32[]{:T(128)}, f32[128,256]{0,1:T(8,128)S(1)}, s32[]{:T(128)}, s32[]{:T(128)}, bf16[3,128,512]{1,2,0:T(8,128)(2,1)S(1)}, /*index=5*/bf16[3,128,128...) while((s32[]{:T(128)}, f32[128,256]{0,1:T(8,128)S(1)}, ...), condition=%wide.region_10.11_spmd, body=%wide.region_9.10_spmd.sunk | while | flops 25280520 | bytes 1442055 | solution.py:153
  27.2 1.3 %collective-permute-start = (f32[128,256]{0,1:T(8,128)S(1)}, f32[128,256]{0,1:T(8,128)S(1)}, u32[]{:S(2)}, u32[]{:S(2)}) collective-permute-start(f32[128,256]{0,1:T(8,128)S(1)} %get-tuple-element.309), channel_id=1, source_target_pairs={{8,0},{16,8},{24,16},{9,1},{17,9},{25,17},{10,2},{18,10},{26,18},{... | collective-permute-start | bytes 393224 | tf_op jit(solution)/shard_map/while/body/eval_jaxpr/ppermute | solution.py:16
  28.5 0.2 fusion.85
  28.7 0.2 convolution_bitcast_fusion.5
  28.9 1.5 %collective-permute-done = f32[128,256]{0,1:T(8,128)S(1)} collective-permute-done((f32[128,256]{0,1:T(8,128)S(1)}, f32[128,256]{0,1:T(8,128)S(1)}, u32[]{:S(2)}, u32[]{:S(2)}) %collective-permute-start) | collective-permute-done | bytes 131104 | tf_op jit(solution)/shard_map/while/body/eval_jaxpr/ppermute | solution.py:16
  30.5 1.3 %collective-permute-start = (f32[128,256]{0,1:T(8,128)S(1)}, f32[128,256]{0,1:T(8,128)S(1)}, u32[]{:S(2)}, u32[]{:S(2)}) collective-permute-start(f32[128,256]{0,1:T(8,128)S(1)} %get-tuple-element.309), channel_id=1, source_target_pairs={{8,0},{16,8},{24,16},{9,1},{17,9},{25,17},{10,2},{18,10},{26,18},{... | collective-permute-start | bytes 393224 | tf_op jit(solution)/shard_map/while/body/eval_jaxpr/ppermute | solution.py:16
  31.8 0.2 fusion.85
  32.0 0.2 convolution_bitcast_fusion.5
  32.2 4.8 %collective-permute-done = f32[128,256]{0,1:T(8,128)S(1)} collective-permute-done((f32[128,256]{0,1:T(8,128)S(1)}, f32[128,256]{0,1:T(8,128)S(1)}, u32[]{:S(2)}, u32[]{:S(2)}) %collective-permute-start) | collective-permute-done | bytes 131104 | tf_op jit(solution)/shard_map/while/body/eval_jaxpr/ppermute | solution.py:16
  37.0 1.3 %collective-permute-start = (f32[128,256]{0,1:T(8,128)S(1)}, f32[128,256]{0,1:T(8,128)S(1)}, u32[]{:S(2)}, u32[]{:S(2)}) collective-permute-start(f32[128,256]{0,1:T(8,128)S(1)} %get-tuple-element.309), channel_id=1, source_target_pairs={{8,0},{16,8},{24,16},{9,1},{17,9},{25,17},{10,2},{18,10},{26,18},{... | collective-permute-start | bytes 393224 | tf_op jit(solution)/shard_map/while/body/eval_jaxpr/ppermute | solution.py:16
  38.3 0.2 fusion.85
  38.6 0.2 convolution_bitcast_fusion.5
  38.8 4.6 %collective-permute-done = f32[128,256]{0,1:T(8,128)S(1)} collective-permute-done((f32[128,256]{0,1:T(8,128)S(1)}, f32[128,256]{0,1:T(8,128)S(1)}, u32[]{:S(2)}, u32[]{:S(2)}) %collective-permute-start) | collective-permute-done | bytes 131104 | tf_op jit(solution)/shard_map/while/body/eval_jaxpr/ppermute | solution.py:16
  43.4 1.8 %collective-permute-start.1 = (f32[128,128]{0,1:T(8,128)S(1)}, f32[128,128]{0,1:T(8,128)S(1)}, u32[]{:S(2)}, u32[]{:S(2)}) collective-permute-start(f32[128,128]{0,1:T(8,128)S(1)} %pad_maximum_fusion.5), channel_id=1, source_target_pairs={{0,1},{1,0},{2,3},{3,2},{4,5},{5,4},{6,7},{7,6},{8,9},{9,8},{10,11... | collective-permute-start | bytes 196616 | tf_op jit(solution)/shard_map/ppermute | solution.py:22
  45.2 0.1 copy.92
  45.3 0.1 eq.70
  45.5 0.1 eq.66
  45.6 0.2 fusion.24
  45.9 0.2 fusion.25
  46.1 0.2 fusion.26
  46.3 0.8 %copy.101 = bf16[128,384]{1,0:T(8,128)(2,1)} copy(bf16[128,384]{0,1:T(8,128)(2,1)S(1)} %pad_maximum_fusion.2) | data formatting | bytes 196608
  47.1 1.2 %reduce-window.6 = s32[4,2,128]{2,1,0:T(2,128)S(1)} reduce-window(s32[4,2,128]{2,1,0:T(2,128)S(1)} %compare_convert_fusion, s32[]{:T(128)} %constant.119.clone.1), window={size=1x1x128 pad=0_0x0_0x127_0}, to_apply=%region_11.12 | reduce-window | flops 130048 | bytes 8196 | tf_op jit(solution)/shard_map/reduce-window
  48.3 0.1 slice.56
  48.4 0.1 copy.94
  48.5 0.1 copy.95
  48.6 0.1 copy.100
  48.7 0.1 broadcast_in_dim.54
  48.9 0.1 add_bitcast_fusion
  49.0 0.1 reduce_sum.99
  49.1 0.1 copy.96
  49.2 0.1 convert_reduce_fusion
  49.3 0.1 select_reduce_fusion.3
  49.5 0.6 fusion.56
  50.1 8.0 %all-gather.2.cloned.1.call-done = bf16[128,6144]{1,0:T(8,128)(2,1)} async-done(((bf16[128,768]{1,0:T(8,128)(2,1)}), bf16[128,6144]{1,0:T(8,128)(2,1)}) %all-gather.2.cloned.1.call-update) | async-done | bytes 1572880 | tf_op jit(solution)/shard_map/all_gather | solution.py:167
  58.1 3.4 %fusion.27 = (bf16[1,64,6144]{2,1,0:T(8,128)(2,1)}, f32[64]{0:T(128)}) fusion(f32[64]{0:T(128)S(1)} %select_reduce_fusion.3, bf16[1,64,6144]{2,1,0:T(8,128)(2,1)S(1)} %copy-done.1, bf16[128,6144]{1,0:T(8,128)(2,1)} %all-gather.2.cloned.1.call-done, s32[512,128]{1,0:T(8,128)S(1)} %convert_reduce_fusion, s32[]{:T(128)S(6)} %select_n.119), kind=kOutput, calls=%fused_computation.44 | convolution fusion | flops 103423936 | bytes 3179268 | tf_op jit(solution)/shard_map/dot_general | solution.py:169
  (41 shorter events, 0.5 us)
Async XLA Ops:
  7.2 0.9 %copy-start = (bf16[128,512]{1,0:T(8,128)(2,1)S(1)}, bf16[128,512]{1,0:T(8,128)(2,1)}, u32[]{:S(2)}) copy-start(bf16[128,512]{1,0:T(8,128)(2,1)} %param.13) | copy-start | bytes 393220
  7.2 10.3 %copy-start.5 = (s32[512]{0:T(512)S(1)}, s32[512]{0:T(512)}, u32[]{:S(2)}) copy-start(s32[512]{0:T(512)} %param.17) | copy-start | bytes 6148
  7.2 10.3 %copy-start.2 = (bf16[128,384]{1,0:T(8,128)(2,1)S(1)}, bf16[128,384]{1,0:T(8,128)(2,1)}, u32[]{:S(2)}) copy-start(bf16[128,384]{1,0:T(8,128)(2,1)} %param.12) | copy-start | bytes 294916
  7.2 50.9 %all-gather.2.cloned.1.call-start = ((), (), s32[]{:S(2)}) async-start(), calls=%async_computation | async-start | bytes 1769472 | tf_op jit(solution)/shard_map/all_gather | solution.py:167
  8.1 16.3 %copy-start.4 = (bf16[128,384]{1,0:T(8,128)(2,1)S(1)}, bf16[128,384]{1,0:T(8,128)(2,1)}, u32[]{:S(2)}) copy-start(bf16[128,384]{1,0:T(8,128)(2,1)} %param.15) | copy-start | bytes 294916
  15.5 9.1 %copy-start.3 = (bf16[128,384]{1,0:T(8,128)(2,1)S(1)}, bf16[128,384]{1,0:T(8,128)(2,1)}, u32[]{:S(2)}) copy-start(bf16[128,384]{1,0:T(8,128)(2,1)} %param.16) | copy-start | bytes 294916
  27.2 18.0 %copy-start.6 = (s32[128,2]{0,1:T(2,128)S(1)}, s32[128,2]{0,1:T(2,128)}, u32[]{:S(2)}) copy-start(s32[128,2]{0,1:T(2,128)} %param.20) | copy-start | bytes 3076
  27.2 3.2 %collective-permute-start = (f32[128,256]{0,1:T(8,128)S(1)}, f32[128,256]{0,1:T(8,128)S(1)}, u32[]{:S(2)}, u32[]{:S(2)}) collective-permute-start(f32[128,256]{0,1:T(8,128)S(1)} %get-tuple-element.309), channel_id=1, source_target_pairs={{8,0},{16,8},{24,16},{9,1},{17,9},{25,17},{10,2},{18,10},{26,18},{... | collective-permute-start | bytes 393224 | tf_op jit(solution)/shard_map/while/body/eval_jaxpr/ppermute | solution.py:16
  30.5 6.5 %collective-permute-start = (f32[128,256]{0,1:T(8,128)S(1)}, f32[128,256]{0,1:T(8,128)S(1)}, u32[]{:S(2)}, u32[]{:S(2)}) collective-permute-start(f32[128,256]{0,1:T(8,128)S(1)} %get-tuple-element.309), channel_id=1, source_target_pairs={{8,0},{16,8},{24,16},{9,1},{17,9},{25,17},{10,2},{18,10},{26,18},{... | collective-permute-start | bytes 393224 | tf_op jit(solution)/shard_map/while/body/eval_jaxpr/ppermute | solution.py:16
  37.0 6.3 %collective-permute-start = (f32[128,256]{0,1:T(8,128)S(1)}, f32[128,256]{0,1:T(8,128)S(1)}, u32[]{:S(2)}, u32[]{:S(2)}) collective-permute-start(f32[128,256]{0,1:T(8,128)S(1)} %get-tuple-element.309), channel_id=1, source_target_pairs={{8,0},{16,8},{24,16},{9,1},{17,9},{25,17},{10,2},{18,10},{26,18},{... | collective-permute-start | bytes 393224 | tf_op jit(solution)/shard_map/while/body/eval_jaxpr/ppermute | solution.py:16
  43.3 5.3 %copy-start.7 = (f32[128,2]{0,1:T(2,128)S(1)}, f32[128,2]{0,1:T(2,128)}, u32[]{:S(2)}) copy-start(f32[128,2]{0,1:T(2,128)} %param.19) | copy-start | bytes 3076
  43.4 14.7 %copy-start.1 = (bf16[1,64,6144]{2,1,0:T(8,128)(2,1)S(1)}, bf16[1,64,6144]{2,1,0:T(8,128)(2,1)}, u32[]{:S(2)}) copy-start(bf16[1,64,6144]{2,1,0:T(8,128)(2,1)} %param.21) | copy-start | bytes 2359300
  43.4 6.0 %collective-permute-start.1 = (f32[128,128]{0,1:T(8,128)S(1)}, f32[128,128]{0,1:T(8,128)S(1)}, u32[]{:S(2)}, u32[]{:S(2)}) collective-permute-start(f32[128,128]{0,1:T(8,128)S(1)} %pad_maximum_fusion.5), channel_id=1, source_target_pairs={{0,1},{1,0},{2,3},{3,2},{4,5},{5,4},{6,7},{7,6},{8,9},{9,8},{10,11... | collective-permute-start | bytes 196616 | tf_op jit(solution)/shard_map/ppermute | solution.py:22
Sparse Core Ops, SparseCore 0:
  10.2 47.7 all-gather.1
where the time goes:
time: 68.8 us; the launch traced here: 68.3 us
  waiting for transfers between devices  19.6 us (28%)
  between operations  14.4 us (21%)
  blocking collectives  12.2 us (18%)
  matrix products  8.62 us (13%)
  starting transfers between devices  5.72 us (8%)
  local copies, waits for them, and re-layouts  5.32 us (8%)
  other arithmetic  2.33 us (3%)
    ppermute x3, waiting for transfers between devices, shifted(): return lax.ppermute(x, axis, pairs)  10.9 us
    all_gather x1, waiting for transfers between devices, local(): full_rows = lax.all_gather(row_grad, 'tp', axis=1, tiled=True)  8.01 us
    all_gather x1, blocking collectives, local(): lax.all_gather(own_keys, 'ctx', axis=0, tiled=True)  6.61 us
    all_gather x1, blocking collectives, local(): lax.all_gather(own_values, 'ctx', axis=0, tiled=True)  5.58 us
    ppermute x3, starting transfers between devices, shifted(): return lax.ppermute(x, axis, pairs)  3.88 us
    dot_general x1, matrix products, local(): jnp.dot(my_tokens.astype(jnp.bfloat16), full_rows, preferred_element_type...  3.42 us
    dot_general x3, matrix products, local(): jnp.dot(query_head, window_keys.T, preferred_element_type=jnp.float32)  2.27 us
    unnamed x30, local copies, waits for them, and re-layouts  2.23 us
  transfers between devices with their start and end apart: 5, of which 4 were waited for; matrix products, arithmetic and copies ran while one was open for 19% of the time, Pallas kernels for 0%

commit v1 on v0

v1 whole, which is shorter than its diff:
```python
import functools
import math

import jax
import jax.numpy as jnp
from jax import lax
from jax.experimental import pallas as pl
from jax.experimental.pallas import tpu as pltpu
from jax.sharding import PartitionSpec as P

HD = 128
QH_DEV = 3
F32 = jnp.float32
BF16 = jnp.bfloat16
MESH = pl.DeviceIdType.MESH


def dot(a, b, dims):
    return lax.dot_general(a, b, (dims, ((), ())), preferred_element_type=F32)


def each(count, body):
    if count <= 4:
        for i in range(count):
            body(i)
    else:
        lax.fori_loop(0, count, lambda i, _: (body(i), 0)[1], 0)


def kernel(
    ctx_size,
    tp_size,
    reach,
    chunks,
    q_in,
    k_in,
    v_in,
    do_in,
    o_in,
    docs_in,
    rows_in,
    gates_in,
    ids_in,
    eo_in,
    dq_out,
    dk_out,
    dv_out,
    dgate_out,
    dexp_out,
    q_raw,
    do_raw,
    o_raw,
    docs,
    gates,
    ids,
    eo,
    kv,
    q_s,
    q_half,
    do_s,
    do_half,
    delta,
    score,
    score_max,
    score_sum,
    dq_acc,
    part_send,
    part_own,
    part_recv,
    rows,
    pick,
    slot_gate,
    y_send,
    y_recv,
    gate_acc,
    in_sem,
    rows_in_sem,
    kv_send_sem,
    kv_recv_sem,
    part_send_sem,
    part_recv_sem,
    row_send_sem,
    row_recv_sem,
    y_send_sem,
    y_recv_sem,
):
    c = lax.axis_index("ctx")
    t = lax.axis_index("tp")
    e, y = t // 2, t % 2
    partner = e * 2 + 1 - y
    experts = tp_size // 2
    n = q_in.shape[0]
    cap = eo.shape[0]
    width = rows_in.shape[1]
    piece = width // chunks
    scaling = 1.0 / math.sqrt(HD)
    head_cols = pl.ds(pl.multiple_of(e * HD, HD), HD)

    row_loads = [
        pltpu.make_async_copy(
            rows_in.at[:, pl.ds(k * piece, piece)], rows.at[e, k], rows_in_sem.at[k]
        )
        for k in range(chunks)
    ]
    loads = {
        name: pltpu.make_async_copy(src, dst, in_sem.at[i])
        for i, (name, src, dst) in enumerate(
            (
                ("k", k_in.at[:, head_cols], kv.at[0, 0]),
                ("v", v_in.at[:, head_cols], kv.at[0, 1]),
                ("ids", ids_in, ids),
                ("gates", gates_in, gates),
                ("q", q_in, q_raw),
                ("do", do_in, do_raw),
                ("o", o_in, o_raw),
                ("docs", docs_in, docs),
                ("eo", eo_in.at[0], eo),
            )
        )
    }
    for load in row_loads:
        load.start()
    for load in loads.values():
        load.start()

    barrier = pltpu.get_barrier_semaphore()

    def greet(ctx, tp):
        pl.semaphore_signal(barrier, inc=1, device_id=(ctx, tp), device_id_type=MESH)

    greet(c, partner)

    @pl.when(e > 0)
    def _():
        greet(c, t - 2)

    @pl.when(e < experts - 1)
    def _():
        greet(c, t + 2)

    greeted = 1 + (e > 0).astype(jnp.int32) + (e < experts - 1).astype(jnp.int32)
    for o in range(1, reach + 1):

        @pl.when(c >= o)
        def _():
            greet(c - o, t)
            greet(c - o, partner)

        @pl.when(c + o < ctx_size)
        def _():
            greet(c + o, t)
            greet(c + o, partner)

        greeted += 2 * (c >= o).astype(jnp.int32) + 2 * (c + o < ctx_size).astype(jnp.int32)
    pl.semaphore_wait(barrier, greeted)

    def row_copy(way, src_e, k):
        to = t + 2 if way == 0 else t - 2
        return pltpu.make_async_remote_copy(
            src_ref=rows.at[src_e, k],
            dst_ref=rows.at[src_e, k],
            send_sem=row_send_sem.at[way, src_e, k],
            recv_sem=row_recv_sem.at[src_e, k],
            device_id=(c, to),
            device_id_type=MESH,
        )

    def y_copy(src_e, k):
        return pltpu.make_async_remote_copy(
            src_ref=y_send.at[src_e, k],
            dst_ref=y_recv.at[src_e, k],
            send_sem=y_send_sem.at[src_e, k],
            recv_sem=y_recv_sem.at[src_e, k],
            device_id=(c, partner),
            device_id_type=MESH,
        )

    def kv_copy(o):
        return pltpu.make_async_remote_copy(
            src_ref=kv.at[0],
            dst_ref=kv.at[o],
            send_sem=kv_send_sem.at[o],
            recv_sem=kv_recv_sem.at[o],
            device_id=(c + o, t),
            device_id_type=MESH,
        )

    def part_copy(o, which):
        return pltpu.make_async_remote_copy(
            src_ref=part_send.at[o, which],
            dst_ref=part_recv.at[o, which],
            send_sem=part_send_sem.at[o, which],
            recv_sem=part_recv_sem.at[o, which],
            device_id=(c - o, t if which == 0 else partner),
            device_id_type=MESH,
        )

    for k in range(chunks):
        row_loads[k].wait()

        @pl.when(e < experts - 1)
        def _():
            row_copy(0, e, k).start()

        @pl.when(e > 0)
        def _():
            row_copy(1, e, k).start()

    loads["k"].wait()
    loads["v"].wait()
    for o in range(1, reach + 1):

        @pl.when(c + o < ctx_size)
        def _():
            kv_copy(o).start()

    loads["ids"].wait()
    loads["gates"].wait()
    named = ids[...] == e
    hit = jnp.sum(jnp.where(named, 1.0, 0.0), axis=1, keepdims=True)
    gate = jnp.sum(jnp.where(named, gates[...], 0.0), axis=1, keepdims=True)
    row_i = lax.broadcasted_iota(jnp.int32, (n, n), 0)
    col_i = lax.broadcasted_iota(jnp.int32, (n, n), 1)
    before = jnp.where(col_i < row_i, 1.0, 0.0).astype(BF16)
    rank = dot(before, jnp.broadcast_to(hit, (n, 2 * cap)).astype(BF16), ((1,), (0,)))
    slot = lax.broadcasted_iota(jnp.int32, (n, 2 * cap), 1)
    slot = jnp.where(slot < cap, slot + cap * y, slot - cap * y).astype(F32)
    chosen = jnp.where(rank == slot, hit, 0.0)
    pick[...] = chosen.T.astype(BF16)
    slot_gate[...] = jnp.sum((chosen * gate).T, axis=1, keepdims=True)[:cap]
    gate_acc[...] = jnp.zeros_like(gate_acc)

    def finish(src, k, routed):
        cols = pl.ds(pl.multiple_of(src * width + k * piece, HD), piece)
        product = routed * eo[:, cols].astype(F32)
        total = gate_acc[...]
        for i in range(piece // HD):
            total += product[:, i * HD : (i + 1) * HD]
        gate_acc[...] = total
        dexp_out[0, :, cols] = (slot_gate[...] * routed).astype(BF16)

    def take(src_e, k):
        picked = dot(pick[...], rows[src_e, k], ((1,), (0,)))
        y_send[src_e, k] = picked[cap:].astype(BF16)
        y_copy(src_e, k).start()
        finish(src_e * 2 + y, k, picked[:cap])

    def take_other(src_e, k):
        y_copy(src_e, k).wait_recv()
        finish(src_e * 2 + 1 - y, k, y_recv[src_e, k].astype(F32))

    loads["eo"].wait()
    for k in range(chunks):
        take(e, k)

    loads["q"].wait()
    loads["do"].wait()
    loads["o"].wait()
    loads["docs"].wait()
    for h in range(QH_DEV):
        at, cols = slice(h * n, (h + 1) * n), slice(h * HD, (h + 1) * HD)
        query, grad, output = q_raw[:, cols], do_raw[:, cols], o_raw[:, cols]
        q_s[at] = query
        do_s[at] = grad
        query, grad = query.astype(F32), grad.astype(F32)
        delta[at] = jnp.sum(grad * output.astype(F32), axis=1, keepdims=True)
        q_half[at] = jnp.where(y == 0, query, pltpu.roll(query, HD // 2, 1)).astype(BF16)
        do_half[at] = jnp.where(y == 1, grad, pltpu.roll(grad, HD // 2, 1)).astype(BF16)

    q_docs = jnp.broadcast_to(docs[pl.ds(c, 1), :].astype(F32), (n, n)).T
    score_max[...] = jnp.full_like(score_max, -1e30)
    score_sum[...] = jnp.zeros_like(score_sum)
    dq_acc[...] = jnp.zeros_like(dq_acc)

    def scores_of(o):
        present = c >= o

        @pl.when(jnp.logical_and(o > 0, present))
        def _():
            kv_copy(o).wait_recv()

        @pl.when(jnp.logical_not(present))
        def _():
            kv[o] = jnp.zeros(kv.shape[1:], BF16)

        k_docs = docs[pl.ds(jnp.maximum(c - o, 0), 1), :].astype(F32)
        allowed = (k_docs == q_docs) & (col_i - o * n <= row_i) & present
        s = dot(q_s[...], kv[o, 0], ((1,), (1,))) * scaling
        s = jnp.where(jnp.concatenate([allowed] * QH_DEV, axis=0), s, -1e30)
        score[o] = s
        score_max[...] = jnp.maximum(score_max[...], s)

    each(reach + 1, scores_of)
    row_max = jnp.max(score_max[...], axis=1, keepdims=True)
    score_max[...] = jnp.broadcast_to(row_max, score_max.shape)

    def exp_of(o):
        p = jnp.exp(score[o] - score_max[...])
        score[o] = p
        score_sum[...] += p

    each(reach + 1, exp_of)
    inverse = 1.0 / jnp.sum(score_sum[...], axis=1, keepdims=True)
    score_sum[...] = jnp.broadcast_to(inverse, score_sum.shape)
    low = lax.broadcasted_iota(jnp.int32, (n, HD), 1) < HD // 2

    def grads_of(i):
        o = reach - i
        probs = score[o] * score_sum[...]
        prob_grad = dot(do_s[...], kv[o, 1], ((1,), (1,)))
        score_grad = (probs * (prob_grad - delta[...])).astype(BF16)
        dq_acc[...] += dot(score_grad, kv[o, 0], ((1,), (0,)))
        dk = dot(score_grad, q_half[...], ((0,), (0,))) * scaling
        dv = dot(probs.astype(BF16), do_half[...], ((0,), (0,)))
        own, other = jnp.where(low, dk, dv), jnp.where(low, dv, dk)
        part_send[o, 1] = other.astype(BF16)

        @pl.when(o == 0)
        def _():
            part_own[...] = own

        @pl.when(jnp.logical_and(o > 0, c >= o))
        def _():
            part_send[o, 0] = own.astype(BF16)
            part_copy(o, 0).start()

        @pl.when(c >= o)
        def _():
            part_copy(o, 1).start()

    each(reach + 1, grads_of)
    for h in range(QH_DEV):
        dq_out[:, h * HD : (h + 1) * HD] = (dq_acc[h * n : (h + 1) * n] * scaling).astype(BF16)

    def sources(step):
        return ((0, e - step, e >= step), (1, e + step, e + step < experts))

    def arrive(step):
        for k in range(chunks):
            for way, src_e, present in sources(step):

                @pl.when(present)
                def _():
                    row_copy(way, src_e, k).wait_recv()

                    @pl.when(e < experts - 1 if way == 0 else e > 0)
                    def _():
                        row_copy(way, src_e, k).start()

                    take(src_e, k)

    def arrive_other(step):
        for k in range(chunks):
            if step == 0:
                take_other(e, k)
                continue
            for _way, src_e, present in sources(step):

                @pl.when(present)
                def _():
                    take_other(src_e, k)

    def sum_parts():
        kept, other = part_own[...], None
        part_copy(0, 1).wait_recv()
        part_own[...] = kept + pltpu.roll(part_recv[0, 1].astype(F32), HD // 2, 1)
        for o in range(1, reach + 1):

            @pl.when(c + o < ctx_size)
            def _():
                part_copy(o, 0).wait_recv()
                part_copy(o, 1).wait_recv()
                part_own[...] += part_recv[o, 0].astype(F32) + pltpu.roll(
                    part_recv[o, 1].astype(F32), HD // 2, 1
                )

        summed = part_own[...].astype(BF16)
        dk_out[...] = summed[:, : HD // 2]
        dv_out[...] = summed[:, HD // 2 :]

    for step in range(1, experts):
        arrive(step)
        arrive_other(step - 1)
        if step == max(1, experts - 2):
            sum_parts()
    arrive_other(experts - 1)

    gate_sum = jnp.sum(gate_acc[...], axis=1, keepdims=True)
    dgate_out[...] = jnp.broadcast_to(gate_sum, (cap, HD)).T[:1]

    for k in range(chunks):

        @pl.when(e < experts - 1)
        def _():
            row_copy(0, e, k).wait_send()

        @pl.when(e > 0)
        def _():
            row_copy(1, e, k).wait_send()

        y_copy(e, k).wait_send()
        for step in range(1, experts):
            for way, src_e, present in sources(step):

                @pl.when(present)
                def _():
                    y_copy(src_e, k).wait_send()

                    @pl.when(e < experts - 1 if way == 0 else e > 0)
                    def _():
                        row_copy(way, src_e, k).wait_send()

    part_copy(0, 1).wait_send()
    for o in range(1, reach + 1):

        @pl.when(c + o < ctx_size)
        def _():
            kv_copy(o).wait_send()

        @pl.when(c >= o)
        def _():
            part_copy(o, 0).wait_send()
            part_copy(o, 1).wait_send()


def local(
    queries,
    key_rows,
    value_rows,
    out_grad,
    attn_out,
    doc_ids,
    row_grad,
    gate_weights,
    expert_ids,
    expert_out,
):
    ctx_size, tp_size = lax.axis_size("ctx"), lax.axis_size("tp")
    n, width = row_grad.shape
    cap, features = expert_out.shape[1:]
    experts = tp_size // 2
    reach = min((doc_ids.shape[0] // 2 + n) // n, ctx_size - 1)
    chunks = 3 if width % (3 * HD) == 0 else 1
    piece = width // chunks
    blocks = reach + 1
    stacked = QH_DEV * n
    dma = pltpu.SemaphoreType.DMA
    return pl.pallas_call(
        functools.partial(kernel, ctx_size, tp_size, reach, chunks),
        out_shape=(
            jax.ShapeDtypeStruct(queries.shape, BF16),
            jax.ShapeDtypeStruct((n, HD // 2), BF16),
            jax.ShapeDtypeStruct((n, HD // 2), BF16),
            jax.ShapeDtypeStruct((1, cap), F32),
            jax.ShapeDtypeStruct(expert_out.shape, BF16),
        ),
        in_specs=[pl.BlockSpec(memory_space=pl.ANY)] * 10,
        out_specs=[pl.BlockSpec(memory_space=pltpu.VMEM)] * 5,
        scratch_shapes=[
            pltpu.VMEM(queries.shape, BF16),
            pltpu.VMEM(queries.shape, BF16),
            pltpu.VMEM(queries.shape, BF16),
            pltpu.VMEM((doc_ids.shape[0] // n, n), jnp.int32),
            pltpu.VMEM(gate_weights.shape, F32),
            pltpu.VMEM(expert_ids.shape, jnp.int32),
            pltpu.VMEM((cap, features), BF16),
            pltpu.VMEM((blocks, 2, n, HD), BF16),
            pltpu.VMEM((stacked, HD), BF16),
            pltpu.VMEM((stacked, HD), BF16),
            pltpu.VMEM((stacked, HD), BF16),
            pltpu.VMEM((stacked, HD), BF16),
            pltpu.VMEM((stacked, 1), F32),
            pltpu.VMEM((blocks, stacked, n), F32),
            pltpu.VMEM((stacked, n), F32),
            pltpu.VMEM((stacked, n), F32),
            pltpu.VMEM((stacked, HD), F32),
            pltpu.VMEM((blocks, 2, n, HD), BF16),
            pltpu.VMEM((n, HD), F32),
            pltpu.VMEM((blocks, 2, n, HD), BF16),
            pltpu.VMEM((experts, chunks, n, piece), BF16),
            pltpu.VMEM((2 * cap, n), BF16),
            pltpu.VMEM((cap, 1), F32),
            pltpu.VMEM((experts, chunks, cap, piece), BF16),
            pltpu.VMEM((experts, chunks, cap, piece), BF16),
            pltpu.VMEM((cap, HD), F32),
            dma((9,)),
            dma((chunks,)),
            dma((blocks,)),
            dma((blocks,)),
            dma((blocks, 2)),
            dma((blocks, 2)),
            dma((2, experts, chunks)),
            dma((experts, chunks)),
            dma((experts, chunks)),
            dma((experts, chunks)),
        ],
        compiler_params=pltpu.CompilerParams(
            collective_id=0, has_side_effects=True, vmem_limit_bytes=40 * 1024 * 1024
        ),
        name="backward",
    )(
        queries,
        key_rows,
        value_rows,
        out_grad,
        attn_out,
        doc_ids.reshape(-1, n),
        row_grad,
        gate_weights,
        expert_ids,
        expert_out,
    )


def solution(mesh):
    in_specs = (
        P("ctx", "tp"),
        P("ctx", None),
        P("ctx", None),
        P("ctx", "tp"),
        P("ctx", "tp"),
        P(),
        P("ctx", "tp"),
        P("ctx", None),
        P("ctx", None),
        P("ctx", "tp", None),
    )
    out_specs = (
        P("ctx", "tp"),
        P("ctx", "tp"),
        P("ctx", "tp"),
        P("ctx", "tp"),
        P("ctx", "tp", None),
    )
    return jax.shard_map(local, mesh=mesh, in_specs=in_specs, out_specs=out_specs, check_vma=False)
```

time: 68.8 us -> 36 us (0.52)
  the two profiles are of different devices: /device:TPU:0 before, /device:TPU:2 now
where the time goes in v1:
time: 36 us; the launch traced here: 35.7 us
  Pallas kernels  24.3 us (68%)
  local copies, waits for them, and re-layouts  10.6 us (29%)
  between operations  0.69 us (2%)
    pallas_call x1, Pallas kernels, local(): pl.pallas_call(functools.partial(kernel, ctx_size, tp_size, reach, chunks...  24.3 us
    unnamed x23, local copies, waits for them, and re-layouts  9.24 us
    pallas_call x2, local copies, waits for them, and re-layouts, local(): pl.pallas_call(functools.partial(kernel, ctx_size, tp_size, reach, chunks...  1.39 us

profile of v1, /device:TPU:2, one launch (start us, length us, event | category | flops | bytes accessed | tf_op | source)
XLA Modules:
  0.0 35.7 jit_solution(716451274147325863)
XLA Ops:
  0.6 0.0 copy-start.8
  0.6 0.0 copy-start.2
  0.7 0.7 %copy-done.8 = f32[128,2]{0,1:T(2,128)S(1)} copy-done((f32[128,2]{0,1:T(2,128)S(1)}, f32[128,2]{0,1:T(2,128)}, u32[]{:S(2)}) %copy-start.8) | copy-done | bytes 1048
  1.3 0.1 copy.15.gates_in
  1.4 0.0 copy-start.7
  1.4 0.8 %copy.16.ids_in = s32[128,2]{1,0:T(8,128)S(1)} copy(s32[128,2]{0,1:T(2,128)} %param.18) | data formatting | bytes 2048 | tf_op args[8]
  2.2 0.0 copy-done.2
  2.2 0.0 copy-done.7
  2.2 0.0 copy-start
  2.3 1.1 %copy-done = bf16[1,64,6144]{2,1,0:T(8,128)(2,1)S(1)} copy-done((bf16[1,64,6144]{2,1,0:T(8,128)(2,1)S(1)}, bf16[1,64,6144]{2,1,0:T(8,128)(2,1)}, u32[]{:S(2)}) %copy-start) | copy-done | bytes 786456
  3.4 0.0 copy-start.1
  3.4 0.9 %copy-done.1 = bf16[128,768]{1,0:T(8,128)(2,1)S(1)} copy-done((bf16[128,768]{1,0:T(8,128)(2,1)S(1)}, bf16[128,768]{1,0:T(8,128)(2,1)}, u32[]{:S(2)}) %copy-start.1) | copy-done | bytes 196632
  4.3 0.0 copy-start.3
  4.3 0.9 %copy-done.3 = bf16[128,512]{1,0:T(8,128)(2,1)S(1)} copy-done((bf16[128,512]{1,0:T(8,128)(2,1)S(1)}, bf16[128,512]{1,0:T(8,128)(2,1)}, u32[]{:S(2)}) %copy-start.3) | copy-done | bytes 131096
  5.2 0.0 copy-start.4
  5.2 0.9 %copy-done.4 = bf16[128,384]{1,0:T(8,128)(2,1)S(1)} copy-done((bf16[128,384]{1,0:T(8,128)(2,1)S(1)}, bf16[128,384]{1,0:T(8,128)(2,1)}, u32[]{:S(2)}) %copy-start.4) | copy-done | bytes 98328
  6.1 0.0 copy-start.5
  6.1 0.9 %copy-done.5 = bf16[128,384]{1,0:T(8,128)(2,1)S(1)} copy-done((bf16[128,384]{1,0:T(8,128)(2,1)S(1)}, bf16[128,384]{1,0:T(8,128)(2,1)}, u32[]{:S(2)}) %copy-start.5) | copy-done | bytes 98328
  7.0 0.0 copy-start.6
  7.0 0.9 %copy-done.6 = bf16[128,384]{1,0:T(8,128)(2,1)S(1)} copy-done((bf16[128,384]{1,0:T(8,128)(2,1)S(1)}, bf16[128,384]{1,0:T(8,128)(2,1)}, u32[]{:S(2)}) %copy-start.6) | copy-done | bytes 98328
  7.9 24.3 %backward.1 = (bf16[128,384]{1,0:T(8,128)(2,1)S(1)}, bf16[128,64]{1,0:T(8,128)(2,1)S(1)}, bf16[128,64]{1,0:T(8,128)(2,1)S(1)}, f32[1,64]{1,0:T(1,128)S(1)}, bf16[1,64,6144]{2,1,0:T(8,128)(2,1)S(1)}) custom-call(bf16[128,384]{1,0:T(8,128)(2,1)S(1)} %copy-done.4, bf16[128,512]{1,0:T(8,128)(2,1)S(1)} %copy-done.2, bf16[128,512]{1,0:T(8,128)(2,1)S(1)} %copy-done.3, ...), custom_call_target="tpu_custom_call" | custom-call | tf_op jit(solution)/shard_map/backward/pallas_call | solution.py:448
  32.2 0.7 %copy.17 = bf16[128,64]{0,1:T(8,128)(2,1)} copy(bf16[128,64]{1,0:T(8,128)(2,1)S(1)} %get-tuple-element.6) | data formatting | bytes 32768 | tf_op jit(solution)/shard_map/backward/pallas_call | solution.py:448
  32.9 0.7 %copy.18 = bf16[128,64]{0,1:T(8,128)(2,1)} copy(bf16[128,64]{1,0:T(8,128)(2,1)S(1)} %get-tuple-element.7) | data formatting | bytes 32768 | tf_op jit(solution)/shard_map/backward/pallas_call | solution.py:448
  33.6 0.6 %copy.22 = bf16[128,384]{1,0:T(8,128)(2,1)} copy(bf16[128,384]{1,0:T(8,128)(2,1)S(1)} %get-tuple-element.15) | data formatting | bytes 196608
  34.3 0.5 %copy.23 = f32[1,64]{1,0:T(1,128)} copy(f32[1,64]{1,0:T(1,128)S(1)} %get-tuple-element.18) | data formatting | bytes 512
  34.8 0.9 %copy.24 = bf16[1,64,6144]{2,1,0:T(8,128)(2,1)} copy(bf16[1,64,6144]{2,1,0:T(8,128)(2,1)S(1)} %get-tuple-element.19) | data formatting | bytes 1572864
Async XLA Ops:
  0.6 0.7 %copy-start.8 = (f32[128,2]{0,1:T(2,128)S(1)}, f32[128,2]{0,1:T(2,128)}, u32[]{:S(2)}) copy-start(f32[128,2]{0,1:T(2,128)} %param.17) | copy-start | bytes 3076
  0.6 1.6 %copy-start.2 = (bf16[128,512]{1,0:T(8,128)(2,1)S(1)}, bf16[128,512]{1,0:T(8,128)(2,1)}, u32[]{:S(2)}) copy-start(bf16[128,512]{1,0:T(8,128)(2,1)} %k_in.1) | copy-start | bytes 393220
  1.4 0.8 %copy-start.7 = (s32[512]{0:T(512)S(1)}, s32[512]{0:T(512)}, u32[]{:S(2)}) copy-start(s32[512]{0:T(512)} %param.15) | copy-start | bytes 6148
  2.2 1.1 %copy-start = (bf16[1,64,6144]{2,1,0:T(8,128)(2,1)S(1)}, bf16[1,64,6144]{2,1,0:T(8,128)(2,1)}, u32[]{:S(2)}) copy-start(bf16[1,64,6144]{2,1,0:T(8,128)(2,1)} %eo_in.1) | copy-start | bytes 2359300
  3.4 0.9 %copy-start.1 = (bf16[128,768]{1,0:T(8,128)(2,1)S(1)}, bf16[128,768]{1,0:T(8,128)(2,1)}, u32[]{:S(2)}) copy-start(bf16[128,768]{1,0:T(8,128)(2,1)} %rows_in.1) | copy-start | bytes 589828
  4.3 0.9 %copy-start.3 = (bf16[128,512]{1,0:T(8,128)(2,1)S(1)}, bf16[128,512]{1,0:T(8,128)(2,1)}, u32[]{:S(2)}) copy-start(bf16[128,512]{1,0:T(8,128)(2,1)} %v_in.1) | copy-start | bytes 393220
  5.2 0.9 %copy-start.4 = (bf16[128,384]{1,0:T(8,128)(2,1)S(1)}, bf16[128,384]{1,0:T(8,128)(2,1)}, u32[]{:S(2)}) copy-start(bf16[128,384]{1,0:T(8,128)(2,1)} %q_in.1) | copy-start | bytes 294916
  6.1 0.9 %copy-start.5 = (bf16[128,384]{1,0:T(8,128)(2,1)S(1)}, bf16[128,384]{1,0:T(8,128)(2,1)}, u32[]{:S(2)}) copy-start(bf16[128,384]{1,0:T(8,128)(2,1)} %do_in.1) | copy-start | bytes 294916
  7.0 0.9 %copy-start.6 = (bf16[128,384]{1,0:T(8,128)(2,1)S(1)}, bf16[128,384]{1,0:T(8,128)(2,1)}, u32[]{:S(2)}) copy-start(bf16[128,384]{1,0:T(8,128)(2,1)} %o_in.1) | copy-start | bytes 294916

commit v2 on v1

--- a/solution.py
+++ b/solution.py
@@ -13,6 +13,7 @@
 F32 = jnp.float32
 BF16 = jnp.bfloat16
 MESH = pl.DeviceIdType.MESH
+VMEM = 62 * 1024 * 1024
 
 
 def dot(a, b, dims):
@@ -42,6 +43,11 @@
     gates_in,
     ids_in,
     eo_in,
+    dq_hbm,
+    dk_hbm,
+    dv_hbm,
+    dgate_hbm,
+    dexp_hbm,
     dq_out,
     dk_out,
     dv_out,
@@ -83,6 +89,8 @@
     row_recv_sem,
     y_send_sem,
     y_recv_sem,
+    out_sem,
+    dexp_sem,
 ):
     c = lax.axis_index("ctx")
     t = lax.axis_index("tp")
@@ -217,18 +225,33 @@
     loads["ids"].wait()
     loads["gates"].wait()
     named = ids[...] == e
-    hit = jnp.sum(jnp.where(named, 1.0, 0.0), axis=1, keepdims=True)
-    gate = jnp.sum(jnp.where(named, gates[...], 0.0), axis=1, keepdims=True)
+    hit = jnp.sum(jnp.where(named, 1.0, 0.0), axis=0, keepdims=True)
+    gate = jnp.sum(jnp.where(named, gates[...], 0.0), axis=0, keepdims=True)
+    hit = jnp.broadcast_to(hit, (2 * cap, n)).T
     row_i = lax.broadcasted_iota(jnp.int32, (n, n), 0)
     col_i = lax.broadcasted_iota(jnp.int32, (n, n), 1)
     before = jnp.where(col_i < row_i, 1.0, 0.0).astype(BF16)
-    rank = dot(before, jnp.broadcast_to(hit, (n, 2 * cap)).astype(BF16), ((1,), (0,)))
+    rank = dot(before, hit.astype(BF16), ((1,), (0,)))
     slot = lax.broadcasted_iota(jnp.int32, (n, 2 * cap), 1)
     slot = jnp.where(slot < cap, slot + cap * y, slot - cap * y).astype(F32)
     chosen = jnp.where(rank == slot, hit, 0.0)
-    pick[...] = chosen.T.astype(BF16)
-    slot_gate[...] = jnp.sum((chosen * gate).T, axis=1, keepdims=True)[:cap]
+    chosen = chosen.T
+    pick[...] = chosen.astype(BF16)
+    slot_gate[...] = jnp.sum(chosen * gate, axis=1, keepdims=True)[:cap]
     gate_acc[...] = jnp.zeros_like(gate_acc)
+
+    def dexp_copy(src, k):
+        cols = pl.ds(pl.multiple_of(src * width + k * piece, HD), piece)
+        return pltpu.make_async_copy(
+            dexp_out.at[:, cols], dexp_hbm.at[0, :, cols], dexp_sem.at[src, k]
+        )
+
+    out_copies = [
+        pltpu.make_async_copy(source, target, out_sem.at[i])
+        for i, (source, target) in enumerate(
+            ((dq_out, dq_hbm), (dk_out, dk_hbm), (dv_out, dv_hbm), (dgate_out, dgate_hbm))
+        )
+    ]
 
     def finish(src, k, routed):
         cols = pl.ds(pl.multiple_of(src * width + k * piece, HD), piece)
@@ -237,7 +260,8 @@
         for i in range(piece // HD):
             total += product[:, i * HD : (i + 1) * HD]
         gate_acc[...] = total
-        dexp_out[0, :, cols] = (slot_gate[...] * routed).astype(BF16)
+        dexp_out[:, cols] = (slot_gate[...] * routed).astype(BF16)
+        dexp_copy(src, k).start()
 
     def take(src_e, k):
         picked = dot(pick[...], rows[src_e, k], ((1,), (0,)))
@@ -273,23 +297,23 @@
     dq_acc[...] = jnp.zeros_like(dq_acc)
 
     def scores_of(o):
-        present = c >= o
-
-        @pl.when(jnp.logical_and(o > 0, present))
-        def _():
-            kv_copy(o).wait_recv()
-
-        @pl.when(jnp.logical_not(present))
-        def _():
-            kv[o] = jnp.zeros(kv.shape[1:], BF16)
-
         k_docs = docs[pl.ds(jnp.maximum(c - o, 0), 1), :].astype(F32)
-        allowed = (k_docs == q_docs) & (col_i - o * n <= row_i) & present
+        allowed = (k_docs == q_docs) & (col_i - o * n <= row_i) & (c >= o)
         s = dot(q_s[...], kv[o, 0], ((1,), (1,))) * scaling
         s = jnp.where(jnp.concatenate([allowed] * QH_DEV, axis=0), s, -1e30)
         score[o] = s
         score_max[...] = jnp.maximum(score_max[...], s)
 
+    for o in range(1, reach + 1):
+
+        @pl.when(c >= o)
+        def _():
+            kv_copy(o).wait_recv()
+
+        @pl.when(c < o)
+        def _():
+            kv[o] = jnp.zeros(kv.shape[1:], BF16)
+
     each(reach + 1, scores_of)
     row_max = jnp.max(score_max[...], axis=1, keepdims=True)
     score_max[...] = jnp.broadcast_to(row_max, score_max.shape)
@@ -304,49 +328,79 @@
     score_sum[...] = jnp.broadcast_to(inverse, score_sum.shape)
     low = lax.broadcasted_iota(jnp.int32, (n, HD), 1) < HD // 2
 
-    def grads_of(i):
-        o = reach - i
+    def grads_of(o):
         probs = score[o] * score_sum[...]
         prob_grad = dot(do_s[...], kv[o, 1], ((1,), (1,)))
         score_grad = (probs * (prob_grad - delta[...])).astype(BF16)
         dq_acc[...] += dot(score_grad, kv[o, 0], ((1,), (0,)))
         dk = dot(score_grad, q_half[...], ((0,), (0,))) * scaling
         dv = dot(probs.astype(BF16), do_half[...], ((0,), (0,)))
-        own, other = jnp.where(low, dk, dv), jnp.where(low, dv, dk)
-        part_send[o, 1] = other.astype(BF16)
-
-        @pl.when(o == 0)
-        def _():
+        own = jnp.where(low, dk, dv)
+        part_send[o, 1] = jnp.where(low, dv, dk).astype(BF16)
+        if isinstance(o, int) and o == 0:
             part_own[...] = own
-
-        @pl.when(jnp.logical_and(o > 0, c >= o))
-        def _():
+        else:
             part_send[o, 0] = own.astype(BF16)
+
+    def send_parts(o):
+        @pl.when(c >= o)
+        def _():
             part_copy(o, 0).start()
-
-        @pl.when(c >= o)
-        def _():
             part_copy(o, 1).start()
 
-    each(reach + 1, grads_of)
+    def forward(step, k):
+        for way, src_e, present in sources(step):
+
+            @pl.when(present)
+            def _():
+                row_copy(way, src_e, k).wait_recv()
+
+                @pl.when(e < experts - 1 if way == 0 else e > 0)
+                def _():
+                    row_copy(way, src_e, k).start()
+
+    def sources(step):
+        return ((0, e - step, e >= step), (1, e + step, e + step < experts))
+
+    early = 0
+    if reach <= 3:
+        while early < chunks - 1:
+            forward(1, early)
+            early += 1
+        late = list(range(reach, reach // 2, -1))
+        for o in late:
+            grads_of(o)
+        for o in late:
+            send_parts(o)
+        while early < chunks:
+            forward(1, early)
+            early += 1
+        near = list(range(reach // 2, -1, -1))
+        for o in near:
+            grads_of(o)
+        for o in near[:-1]:
+            send_parts(o)
+    else:
+
+        @pl.loop(0, reach)
+        def _(i):
+            grads_of(reach - i)
+            send_parts(reach - i)
+
+        grads_of(0)
+    part_copy(0, 1).start()
     for h in range(QH_DEV):
         dq_out[:, h * HD : (h + 1) * HD] = (dq_acc[h * n : (h + 1) * n] * scaling).astype(BF16)
-
-    def sources(step):
-        return ((0, e - step, e >= step), (1, e + step, e + step < experts))
+    out_copies[0].start()
 
     def arrive(step):
         for k in range(chunks):
-            for way, src_e, present in sources(step):
+            if step > 1 or k >= early:
+                forward(step, k)
+            for _way, src_e, present in sources(step):
 
                 @pl.when(present)
                 def _():
-                    row_copy(way, src_e, k).wait_recv()
-
-                    @pl.when(e < experts - 1 if way == 0 else e > 0)
-                    def _():
-                        row_copy(way, src_e, k).start()
-
                     take(src_e, k)
 
     def arrive_other(step):
@@ -361,9 +415,8 @@
                     take_other(src_e, k)
 
     def sum_parts():
-        kept, other = part_own[...], None
         part_copy(0, 1).wait_recv()
-        part_own[...] = kept + pltpu.roll(part_recv[0, 1].astype(F32), HD // 2, 1)
+        part_own[...] += pltpu.roll(part_recv[0, 1].astype(F32), HD // 2, 1)
         for o in range(1, reach + 1):
 
             @pl.when(c + o < ctx_size)
@@ -374,9 +427,11 @@
                     part_recv[o, 1].astype(F32), HD // 2, 1
                 )
 
-        summed = part_own[...].astype(BF16)
-        dk_out[...] = summed[:, : HD // 2]
-        dv_out[...] = summed[:, HD // 2 :]
+        summed = part_own[...].T.astype(BF16)
+        dk_out[...] = summed[: HD // 2]
+        dv_out[...] = summed[HD // 2 :]
+        out_copies[1].start()
+        out_copies[2].start()
 
     for step in range(1, experts):
         arrive(step)
@@ -387,6 +442,7 @@
 
     gate_sum = jnp.sum(gate_acc[...], axis=1, keepdims=True)
     dgate_out[...] = jnp.broadcast_to(gate_sum, (cap, HD)).T[:1]
+    out_copies[3].start()
 
     for k in range(chunks):
 
@@ -410,6 +466,11 @@
                     def _():
                         row_copy(way, src_e, k).wait_send()
 
+    for copy in out_copies:
+        copy.wait()
+    for src in range(tp_size):
+        for k in range(chunks):
+            dexp_copy(src, k).wait()
     part_copy(0, 1).wait_send()
     for o in range(1, reach + 1):
 
@@ -421,6 +482,22 @@
         def _():
             part_copy(o, 0).wait_send()
             part_copy(o, 1).wait_send()
+
+
+def write(*refs):
+    sources, targets, sem = list(refs[:5]), list(refs[5:10]), refs[10]
+    large_in, large_out = sources.pop(), targets.pop()
+    for row in range(0, large_in.shape[1], 16):
+        sources.append(large_in.at[0, pl.ds(row, 16)])
+        targets.append(large_out.at[0, pl.ds(row, 16)])
+    copies = [
+        pltpu.make_async_copy(source, target, sem.at[i])
+        for i, (source, target) in enumerate(zip(sources, targets))
+    ]
+    for copy in reversed(copies):
+        copy.start()
+    for copy in copies:
+        copy.wait()
 
 
 def local(
@@ -445,24 +522,27 @@
     blocks = reach + 1
     stacked = QH_DEV * n
     dma = pltpu.SemaphoreType.DMA
-    return pl.pallas_call(
+    out_shape = (
+        jax.ShapeDtypeStruct(queries.shape, BF16),
+        jax.ShapeDtypeStruct((HD // 2, n), BF16),
+        jax.ShapeDtypeStruct((HD // 2, n), BF16),
+        jax.ShapeDtypeStruct((1, cap), F32),
+        jax.ShapeDtypeStruct(expert_out.shape, BF16),
+    )
+    outs = pl.pallas_call(
         functools.partial(kernel, ctx_size, tp_size, reach, chunks),
-        out_shape=(
-            jax.ShapeDtypeStruct(queries.shape, BF16),
-            jax.ShapeDtypeStruct((n, HD // 2), BF16),
-            jax.ShapeDtypeStruct((n, HD // 2), BF16),
-            jax.ShapeDtypeStruct((1, cap), F32),
-            jax.ShapeDtypeStruct(expert_out.shape, BF16),
-        ),
-        in_specs=[pl.BlockSpec(memory_space=pl.ANY)] * 10,
-        out_specs=[pl.BlockSpec(memory_space=pltpu.VMEM)] * 5,
+        out_shape=out_shape,
+        in_specs=[pl.BlockSpec(memory_space=pltpu.HBM)] * 10,
+        out_specs=[pl.BlockSpec(memory_space=pltpu.HBM)] * 5,
         scratch_shapes=[
+            *(pltpu.VMEM(out.shape, out.dtype) for out in out_shape[:4]),
+            pltpu.VMEM((cap, features), BF16),
             pltpu.VMEM(queries.shape, BF16),
             pltpu.VMEM(queries.shape, BF16),
             pltpu.VMEM(queries.shape, BF16),
             pltpu.VMEM((doc_ids.shape[0] // n, n), jnp.int32),
-            pltpu.VMEM(gate_weights.shape, F32),
-            pltpu.VMEM(expert_ids.shape, jnp.int32),
+            pltpu.VMEM(gate_weights.shape[::-1], F32),
+            pltpu.VMEM(expert_ids.shape[::-1], jnp.int32),
             pltpu.VMEM((cap, features), BF16),
             pltpu.VMEM((blocks, 2, n, HD), BF16),
             pltpu.VMEM((stacked, HD), BF16),
@@ -493,9 +573,11 @@
             dma((experts, chunks)),
             dma((experts, chunks)),
             dma((experts, chunks)),
+            dma((4,)),
+            dma((tp_size, chunks)),
         ],
         compiler_params=pltpu.CompilerParams(
-            collective_id=0, has_side_effects=True, vmem_limit_bytes=40 * 1024 * 1024
+            collective_id=0, has_side_effects=True, vmem_limit_bytes=VMEM
         ),
         name="backward",
     )(
@@ -506,10 +588,20 @@
         attn_out,
         doc_ids.reshape(-1, n),
         row_grad,
-        gate_weights,
-        expert_ids,
+        gate_weights.T,
+        expert_ids.T,
         expert_out,
     )
+    query_grad, key_grad, value_grad, gate_grad, expert_grad = pl.pallas_call(
+        write,
+        out_shape=out_shape,
+        in_specs=[pl.BlockSpec(memory_space=pltpu.HBM)] * 5,
+        out_specs=[pl.BlockSpec(memory_space=pltpu.HBM)] * 5,
+        scratch_shapes=[dma((4 + cap // 16,))],
+        compiler_params=pltpu.CompilerParams(vmem_limit_bytes=VMEM),
+        name="write",
+    )(*outs)
+    return (query_grad, key_grad.T, value_grad.T, gate_grad, expert_grad)
 
 
 def solution(mesh):

time: 36 us -> 53.9 us (1.50)
  the two profiles are of different devices: /device:TPU:2 before, /device:TPU:0 now
where the time goes in v2:
time: 53.9 us; the launch traced here: 53.7 us
  Pallas kernels  53.1 us (99%)
  between operations  0.64 us (1%)
    pallas_call x1, Pallas kernels, local(): pl.pallas_call(write, out_shape=out_shape, in_specs=[pl.BlockSpec(memory_...  29 us
    pallas_call x1, Pallas kernels, local(): pl.pallas_call(functools.partial(kernel, ctx_size, tp_size, reach, chunks...  24.1 us

profile of v2, /device:TPU:0, one launch (start us, length us, event | category | flops | bytes accessed | tf_op | source)
XLA Modules:
  0.0 53.7 jit_solution(15556779931302742716)
XLA Ops:
  0.6 24.1 %backward.1 = (bf16[128,384]{1,0:T(8,128)(2,1)}, bf16[64,128]{1,0:T(8,128)(2,1)}, bf16[64,128]{1,0:T(8,128)(2,1)}, f32[1,64]{1,0:T(1,128)}, bf16[1,64,6144]{2,1,0:T(8,128)(2,1)}) custom-call(bf16[128,384]{1,0:T(8,128)(2,1)} %q_in.1, bf16[128,512]{1,0:T(8,128)(2,1)} %k_in.1, bf16[128,512]{1,0:T(8,128)(2,1)} %v_in.1, bf16[128,384]{1,0:T(8,128)(2,1)} %do_in.1, ...), custom_call_target="tpu_custom_call" | custom-call | tf_op jit(solution)/shard_map/backward/pallas_call | solution.py:532
  24.7 29.0 %write.1 = (bf16[128,384]{1,0:T(8,128)(2,1)}, bf16[64,128]{1,0:T(8,128)(2,1)}, bf16[64,128]{1,0:T(8,128)(2,1)}, f32[1,64]{1,0:T(1,128)}, bf16[1,64,6144]{2,1,0:T(8,128)(2,1)}) custom-call(bf16[128,384]{1,0:T(8,128)(2,1)} %get-tuple-element.15.refs_0_, bf16[64,128]{1,0:T(8,128)(2,1)} %get-tuple-element.16.refs_1_, bf16[64,128]{1,0:T(8,128)(2,1)} %get-tuple-element.17.refs_2_, ...), custom_call_target="tpu_custom_call" | custom-call | tf_op jit(solution)/shard_map/write/pallas_call | solution.py:595

commit v3 on v2

--- a/solution.py
+++ b/solution.py
@@ -104,9 +104,12 @@
     scaling = 1.0 / math.sqrt(HD)
     head_cols = pl.ds(pl.multiple_of(e * HD, HD), HD)
 
+    def cut(k):
+        return pl.ds(k * piece, piece)
+
     row_loads = [
         pltpu.make_async_copy(
-            rows_in.at[:, pl.ds(k * piece, piece)], rows.at[e, k], rows_in_sem.at[k]
+            rows_in.at[:, cut(k)], rows.at[e, :, cut(k)], rows_in_sem.at[k]
         )
         for k in range(chunks)
     ]
@@ -165,20 +168,27 @@
     def row_copy(way, src_e, k):
         to = t + 2 if way == 0 else t - 2
         return pltpu.make_async_remote_copy(
-            src_ref=rows.at[src_e, k],
-            dst_ref=rows.at[src_e, k],
+            src_ref=rows.at[src_e, :, cut(k)],
+            dst_ref=rows.at[src_e, :, cut(k)],
             send_sem=row_send_sem.at[way, src_e, k],
             recv_sem=row_recv_sem.at[src_e, k],
             device_id=(c, to),
             device_id_type=MESH,
         )
 
-    def y_copy(src_e, k):
+    whole = ((0, width),)
+    pieces = tuple((k * piece, piece) for k in range(chunks))
+
+    def parts_at(step):
+        return pieces if step == experts - 1 else whole
+
+    def y_copy(src_e, part):
+        first, count = part
         return pltpu.make_async_remote_copy(
-            src_ref=y_send.at[src_e, k],
-            dst_ref=y_recv.at[src_e, k],
-            send_sem=y_send_sem.at[src_e, k],
-            recv_sem=y_recv_sem.at[src_e, k],
+            src_ref=y_send.at[src_e, :, pl.ds(first, count)],
+            dst_ref=y_recv.at[src_e, :, pl.ds(first, count)],
+            send_sem=y_send_sem.at[src_e, first // piece],
+            recv_sem=y_recv_sem.at[src_e, first // piece],
             device_id=(c, partner),
             device_id_type=MESH,
         )
@@ -240,10 +250,11 @@
     slot_gate[...] = jnp.sum(chosen * gate, axis=1, keepdims=True)[:cap]
     gate_acc[...] = jnp.zeros_like(gate_acc)
 
-    def dexp_copy(src, k):
-        cols = pl.ds(pl.multiple_of(src * width + k * piece, HD), piece)
+    def dexp_copy(src, part):
+        first, count = part
+        cols = pl.ds(pl.multiple_of(src * width + first, HD), count)
         return pltpu.make_async_copy(
-            dexp_out.at[:, cols], dexp_hbm.at[0, :, cols], dexp_sem.at[src, k]
+            dexp_out.at[:, cols], dexp_hbm.at[0, :, cols], dexp_sem.at[src, first // piece]
         )
 
     out_copies = [
@@ -253,29 +264,33 @@
         )
     ]
 
-    def finish(src, k, routed):
-        cols = pl.ds(pl.multiple_of(src * width + k * piece, HD), piece)
+    def finish(src, part, routed):
+        first, count = part
+        cols = pl.ds(pl.multiple_of(src * width + first, HD), count)
         product = routed * eo[:, cols].astype(F32)
         total = gate_acc[...]
-        for i in range(piece // HD):
+        for i in range(count // HD):
             total += product[:, i * HD : (i + 1) * HD]
         gate_acc[...] = total
         dexp_out[:, cols] = (slot_gate[...] * routed).astype(BF16)
-        dexp_copy(src, k).start()
-
-    def take(src_e, k):
-        picked = dot(pick[...], rows[src_e, k], ((1,), (0,)))
-        y_send[src_e, k] = picked[cap:].astype(BF16)
-        y_copy(src_e, k).start()
-        finish(src_e * 2 + y, k, picked[:cap])
-
-    def take_other(src_e, k):
-        y_copy(src_e, k).wait_recv()
-        finish(src_e * 2 + 1 - y, k, y_recv[src_e, k].astype(F32))
+        dexp_copy(src, part).start()
+
+    def take(src_e, part):
+        first, count = part
+        cols = pl.ds(first, count)
+        picked = dot(pick[...], rows[src_e, :, cols], ((1,), (0,)))
+        y_send[src_e, :, cols] = picked[cap:].astype(BF16)
+        y_copy(src_e, part).start()
+        finish(src_e * 2 + y, part, picked[:cap])
+
+    def take_other(src_e, part):
+        first, count = part
+        y_copy(src_e, part).wait_recv()
+        other = y_recv[src_e, :, pl.ds(first, count)]
+        finish(src_e * 2 + 1 - y, part, other.astype(F32))
 
     loads["eo"].wait()
-    for k in range(chunks):
-        take(e, k)
+    take(e, whole[0])
 
     loads["q"].wait()
     loads["do"].wait()
@@ -394,25 +409,28 @@
     out_copies[0].start()
 
     def arrive(step):
+        todo = parts_at(step)
         for k in range(chunks):
             if step > 1 or k >= early:
                 forward(step, k)
+            if len(todo) == 1 and k < chunks - 1:
+                continue
             for _way, src_e, present in sources(step):
 
                 @pl.when(present)
                 def _():
-                    take(src_e, k)
+                    take(src_e, todo[min(k, len(todo) - 1)])
 
     def arrive_other(step):
-        for k in range(chunks):
-            if step == 0:
-                take_other(e, k)
-                continue
+        if step == 0:
+            take_other(e, whole[0])
+            return
+        for part in parts_at(step):
             for _way, src_e, present in sources(step):
 
                 @pl.when(present)
                 def _():
-                    take_other(src_e, k)
+                    take_other(src_e, part)
 
     def sum_parts():
         part_copy(0, 1).wait_recv()
@@ -444,6 +462,9 @@
     dgate_out[...] = jnp.broadcast_to(gate_sum, (cap, HD)).T[:1]
     out_copies[3].start()
 
+    y_copy(e, whole[0]).wait_send()
+    dexp_copy(e * 2, whole[0]).wait()
+    dexp_copy(e * 2 + 1, whole[0]).wait()
     for k in range(chunks):
 
         @pl.when(e < experts - 1)
@@ -454,23 +475,23 @@
         def _():
             row_copy(1, e, k).wait_send()
 
-        y_copy(e, k).wait_send()
-        for step in range(1, experts):
-            for way, src_e, present in sources(step):
-
-                @pl.when(present)
+    for step in range(1, experts):
+        for way, src_e, present in sources(step):
+
+            @pl.when(present)
+            def _():
+                for part in parts_at(step):
+                    y_copy(src_e, part).wait_send()
+                    dexp_copy(src_e * 2, part).wait()
+                    dexp_copy(src_e * 2 + 1, part).wait()
+
+                @pl.when(e < experts - 1 if way == 0 else e > 0)
                 def _():
-                    y_copy(src_e, k).wait_send()
-
-                    @pl.when(e < experts - 1 if way == 0 else e > 0)
-                    def _():
+                    for k in range(chunks):
                         row_copy(way, src_e, k).wait_send()
 
     for copy in out_copies:
         copy.wait()
-    for src in range(tp_size):
-        for k in range(chunks):
-            dexp_copy(src, k).wait()
     part_copy(0, 1).wait_send()
     for o in range(1, reach + 1):
 
@@ -485,18 +506,21 @@
 
 
 def write(*refs):
-    sources, targets, sem = list(refs[:5]), list(refs[5:10]), refs[10]
-    large_in, large_out = sources.pop(), targets.pop()
-    for row in range(0, large_in.shape[1], 16):
-        sources.append(large_in.at[0, pl.ds(row, 16)])
-        targets.append(large_out.at[0, pl.ds(row, 16)])
-    copies = [
-        pltpu.make_async_copy(source, target, sem.at[i])
-        for i, (source, target) in enumerate(zip(sources, targets))
+    sources, targets, held, sem = refs[:5], refs[5:10], refs[10:15], refs[15]
+    into = [
+        pltpu.make_async_copy(source, hold, sem.at[0, i])
+        for i, (source, hold) in enumerate(zip(sources, held))
     ]
-    for copy in reversed(copies):
+    out = [
+        pltpu.make_async_copy(hold, target, sem.at[1, i])
+        for i, (hold, target) in enumerate(zip(held, targets))
+    ]
+    for copy in into:
         copy.start()
-    for copy in copies:
+    for first, second in zip(into, out):
+        first.wait()
+        second.start()
+    for copy in out:
         copy.wait()
 
 
@@ -517,8 +541,7 @@
     cap, features = expert_out.shape[1:]
     experts = tp_size // 2
     reach = min((doc_ids.shape[0] // 2 + n) // n, ctx_size - 1)
-    chunks = 3 if width % (3 * HD) == 0 else 1
-    piece = width // chunks
+    chunks = 2 if width % (2 * HD) == 0 else 1
     blocks = reach + 1
     stacked = QH_DEV * n
     dma = pltpu.SemaphoreType.DMA
@@ -557,11 +580,11 @@
             pltpu.VMEM((blocks, 2, n, HD), BF16),
             pltpu.VMEM((n, HD), F32),
             pltpu.VMEM((blocks, 2, n, HD), BF16),
-            pltpu.VMEM((experts, chunks, n, piece), BF16),
+            pltpu.VMEM((experts, n, width), BF16),
             pltpu.VMEM((2 * cap, n), BF16),
             pltpu.VMEM((cap, 1), F32),
-            pltpu.VMEM((experts, chunks, cap, piece), BF16),
-            pltpu.VMEM((experts, chunks, cap, piece), BF16),
+            pltpu.VMEM((experts, cap, width), BF16),
+            pltpu.VMEM((experts, cap, width), BF16),
             pltpu.VMEM((cap, HD), F32),
             dma((9,)),
             dma((chunks,)),
@@ -597,7 +620,10 @@
         out_shape=out_shape,
         in_specs=[pl.BlockSpec(memory_space=pltpu.HBM)] * 5,
         out_specs=[pl.BlockSpec(memory_space=pltpu.HBM)] * 5,
-        scratch_shapes=[dma((4 + cap // 16,))],
+        scratch_shapes=[
+            *(pltpu.VMEM(out.shape, out.dtype) for out in out_shape),
+            dma((2, 5)),
+        ],
         compiler_params=pltpu.CompilerParams(vmem_limit_bytes=VMEM),
         name="write",
     )(*outs)

time: 53.9 us -> 27.8 us (0.52)
  Pallas kernels: 53.1 us -> 27 us
    pallas_call x1, Pallas kernels: 29 us -> 2.2 us  [local(): pl.pallas_call(write, out_shape=out_shape, in_specs=[pl.BlockSpec(memory_...]
    pallas_call x1, Pallas kernels: 24.1 us -> 24.8 us  [local(): pl.pallas_call(functools.partial(kernel, ctx_size, tp_size, reach, chunks...]
where the time goes in v3:
time: 27.8 us; the launch traced here: 27.6 us
  Pallas kernels  27 us (97%)
  between operations  0.64 us (2%)
    pallas_call x1, Pallas kernels, local(): pl.pallas_call(functools.partial(kernel, ctx_size, tp_size, reach, chunks...  24.8 us
    pallas_call x1, Pallas kernels, local(): pl.pallas_call(write, out_shape=out_shape, in_specs=[pl.BlockSpec(memory_...  2.2 us

profile of v3, /device:TPU:0, one launch (start us, length us, event | category | flops | bytes accessed | tf_op | source)
XLA Modules:
  0.0 27.6 jit_solution(8669200207257537710)
XLA Ops:
  0.6 24.8 %backward.1 = (bf16[128,384]{1,0:T(8,128)(2,1)}, bf16[64,128]{1,0:T(8,128)(2,1)}, bf16[64,128]{1,0:T(8,128)(2,1)}, f32[1,64]{1,0:T(1,128)}, bf16[1,64,6144]{2,1,0:T(8,128)(2,1)}) custom-call(bf16[128,384]{1,0:T(8,128)(2,1)} %q_in.1, bf16[128,512]{1,0:T(8,128)(2,1)} %k_in.1, bf16[128,512]{1,0:T(8,128)(2,1)} %v_in.1, bf16[128,384]{1,0:T(8,128)(2,1)} %do_in.1, ...), custom_call_target="tpu_custom_call" | custom-call | tf_op jit(solution)/shard_map/backward/pallas_call | solution.py:555
  25.4 2.2 %write.1 = (bf16[128,384]{1,0:T(8,128)(2,1)}, bf16[64,128]{1,0:T(8,128)(2,1)}, bf16[64,128]{1,0:T(8,128)(2,1)}, f32[1,64]{1,0:T(1,128)}, bf16[1,64,6144]{2,1,0:T(8,128)(2,1)}) custom-call(bf16[128,384]{1,0:T(8,128)(2,1)} %get-tuple-element.15.refs_0_, bf16[64,128]{1,0:T(8,128)(2,1)} %get-tuple-element.16.refs_1_, bf16[64,128]{1,0:T(8,128)(2,1)} %get-tuple-element.17.refs_2_, ...), custom_call_target="tpu_custom_call" | custom-call | tf_op jit(solution)/shard_map/write/pallas_call | solution.py:618

commit v4 on v3

--- a/solution.py
+++ b/solution.py
@@ -364,38 +364,38 @@
             part_copy(o, 1).start()
 
     def forward(step, k):
+        if step >= experts:
+            return
         for way, src_e, present in sources(step):
 
-            @pl.when(present)
+            @pl.when(jnp.logical_and(present, passes(way)))
             def _():
                 row_copy(way, src_e, k).wait_recv()
-
-                @pl.when(e < experts - 1 if way == 0 else e > 0)
-                def _():
-                    row_copy(way, src_e, k).start()
+                row_copy(way, src_e, k).start()
+
+    def passes(way):
+        return e < experts - 1 if way == 0 else e > 0
 
     def sources(step):
         return ((0, e - step, e >= step), (1, e + step, e + step < experts))
 
-    early = 0
     if reach <= 3:
-        while early < chunks - 1:
-            forward(1, early)
-            early += 1
         late = list(range(reach, reach // 2, -1))
+        near = list(range(reach // 2, -1, -1))
+        forward(1, 0)
         for o in late:
             grads_of(o)
         for o in late:
             send_parts(o)
-        while early < chunks:
-            forward(1, early)
-            early += 1
-        near = list(range(reach // 2, -1, -1))
+        for k in range(1, chunks):
+            forward(1, k)
         for o in near:
             grads_of(o)
         for o in near[:-1]:
             send_parts(o)
     else:
+        for k in range(chunks):
+            forward(1, k)
 
         @pl.loop(0, reach)
         def _(i):
@@ -409,17 +409,18 @@
     out_copies[0].start()
 
     def arrive(step):
-        todo = parts_at(step)
-        for k in range(chunks):
-            if step > 1 or k >= early:
-                forward(step, k)
-            if len(todo) == 1 and k < chunks - 1:
-                continue
-            for _way, src_e, present in sources(step):
+        for part in parts_at(step):
+            for way, src_e, present in sources(step):
+
+                @pl.when(jnp.logical_and(present, jnp.logical_not(passes(way))))
+                def _():
+                    for k in range(chunks):
+                        if part[0] <= k * piece < part[0] + part[1]:
+                            row_copy(way, src_e, k).wait_recv()
 
                 @pl.when(present)
                 def _():
-                    take(src_e, todo[min(k, len(todo) - 1)])
+                    take(src_e, part)
 
     def arrive_other(step):
         if step == 0:
@@ -452,7 +453,10 @@
         out_copies[2].start()
 
     for step in range(1, experts):
+        forward(step + 1, 0)
         arrive(step)
+        for k in range(1, chunks):
+            forward(step + 1, k)
         arrive_other(step - 1)
         if step == max(1, experts - 2):
             sum_parts()
@@ -507,14 +511,20 @@
 
 def write(*refs):
     sources, targets, held, sem = refs[:5], refs[5:10], refs[10:15], refs[15]
-    into = [
-        pltpu.make_async_copy(source, hold, sem.at[0, i])
-        for i, (source, hold) in enumerate(zip(sources, held))
-    ]
-    out = [
-        pltpu.make_async_copy(hold, target, sem.at[1, i])
-        for i, (hold, target) in enumerate(zip(held, targets))
-    ]
+    into, out = [], []
+
+    def through(source, hold, target):
+        i = len(into)
+        into.append(pltpu.make_async_copy(source, hold, sem.at[0, i]))
+        out.append(pltpu.make_async_copy(hold, target, sem.at[1, i]))
+
+    for source, target, hold in zip(sources, targets, held):
+        if len(source.shape) == 2:
+            through(source, hold, target)
+            continue
+        for row in range(0, source.shape[1], 16):
+            at = pl.ds(row, 16)
+            through(source.at[0, at], hold.at[0, at], target.at[0, at])
     for copy in into:
         copy.start()
     for first, second in zip(into, out):
@@ -622,7 +632,7 @@
         out_specs=[pl.BlockSpec(memory_space=pltpu.HBM)] * 5,
         scratch_shapes=[
             *(pltpu.VMEM(out.shape, out.dtype) for out in out_shape),
-            dma((2, 5)),
+            dma((2, 4 + cap // 16)),
         ],
         compiler_params=pltpu.CompilerParams(vmem_limit_bytes=VMEM),
         name="write",

time: 27.8 us -> 27.7 us (level)
  no operation moved by 1% of the time
where the time goes in v4:
time: 27.7 us; the launch traced here: 27.5 us
  Pallas kernels  26.9 us (97%)
  between operations  0.64 us (2%)
    pallas_call x1, Pallas kernels, local(): pl.pallas_call(functools.partial(kernel, ctx_size, tp_size, reach, chunks...  24.8 us
    pallas_call x1, Pallas kernels, local(): pl.pallas_call(write, out_shape=out_shape, in_specs=[pl.BlockSpec(memory_...  2.09 us

profile of v4, /device:TPU:0, one launch (start us, length us, event | category | flops | bytes accessed | tf_op | source)
XLA Modules:
  0.0 27.5 jit_solution(3855560082982746287)
XLA Ops:
  0.6 24.8 %backward.1 = (bf16[128,384]{1,0:T(8,128)(2,1)}, bf16[64,128]{1,0:T(8,128)(2,1)}, bf16[64,128]{1,0:T(8,128)(2,1)}, f32[1,64]{1,0:T(1,128)}, bf16[1,64,6144]{2,1,0:T(8,128)(2,1)}) custom-call(bf16[128,384]{1,0:T(8,128)(2,1)} %q_in.1, bf16[128,512]{1,0:T(8,128)(2,1)} %k_in.1, bf16[128,512]{1,0:T(8,128)(2,1)} %v_in.1, bf16[128,384]{1,0:T(8,128)(2,1)} %do_in.1, ...), custom_call_target="tpu_custom_call" | custom-call | tf_op jit(solution)/shard_map/backward/pallas_call | solution.py:565
  25.4 2.1 %write.1 = (bf16[128,384]{1,0:T(8,128)(2,1)}, bf16[64,128]{1,0:T(8,128)(2,1)}, bf16[64,128]{1,0:T(8,128)(2,1)}, f32[1,64]{1,0:T(1,128)}, bf16[1,64,6144]{2,1,0:T(8,128)(2,1)}) custom-call(bf16[128,384]{1,0:T(8,128)(2,1)} %get-tuple-element.15.refs_0_, bf16[64,128]{1,0:T(8,128)(2,1)} %get-tuple-element.16.refs_1_, bf16[64,128]{1,0:T(8,128)(2,1)} %get-tuple-element.17.refs_2_, ...), custom_call_target="tpu_custom_call" | custom-call | tf_op jit(solution)/shard_map/write/pallas_call | solution.py:628

commit v5 on v4

--- a/solution.py
+++ b/solution.py
@@ -13,7 +13,7 @@
 F32 = jnp.float32
 BF16 = jnp.bfloat16
 MESH = pl.DeviceIdType.MESH
-VMEM = 62 * 1024 * 1024
+VMEM = 40 * 1024 * 1024
 
 
 def dot(a, b, dims):
@@ -28,11 +28,19 @@
         lax.fori_loop(0, count, lambda i, _: (body(i), 0)[1], 0)
 
 
+def cuts(width):
+    pieces, first, rest = [], 0, width // HD
+    while rest > 0:
+        count = (rest + 1) // 2
+        pieces.append((first * HD, count * HD, len(pieces)))
+        first, rest = first + count, rest - count
+    return pieces
+
+
 def kernel(
     ctx_size,
     tp_size,
     reach,
-    chunks,
     q_in,
     k_in,
     v_in,
@@ -43,11 +51,6 @@
     gates_in,
     ids_in,
     eo_in,
-    dq_hbm,
-    dk_hbm,
-    dv_hbm,
-    dgate_hbm,
-    dexp_hbm,
     dq_out,
     dk_out,
     dv_out,
@@ -89,8 +92,6 @@
     row_recv_sem,
     y_send_sem,
     y_recv_sem,
-    out_sem,
-    dexp_sem,
 ):
     c = lax.axis_index("ctx")
     t = lax.axis_index("tp")
@@ -100,12 +101,13 @@
     n = q_in.shape[0]
     cap = eo.shape[0]
     width = rows_in.shape[1]
-    piece = width // chunks
+    pieces = cuts(width)
+    chunks = len(pieces)
     scaling = 1.0 / math.sqrt(HD)
     head_cols = pl.ds(pl.multiple_of(e * HD, HD), HD)
 
     def cut(k):
-        return pl.ds(k * piece, piece)
+        return pl.ds(*pieces[k][:2])
 
     row_loads = [
         pltpu.make_async_copy(
@@ -176,19 +178,18 @@
             device_id_type=MESH,
         )
 
-    whole = ((0, width),)
-    pieces = tuple((k * piece, piece) for k in range(chunks))
+    whole = ((0, width, 0),)
 
     def parts_at(step):
         return pieces if step == experts - 1 else whole
 
     def y_copy(src_e, part):
-        first, count = part
+        first, count, index = part
         return pltpu.make_async_remote_copy(
             src_ref=y_send.at[src_e, :, pl.ds(first, count)],
             dst_ref=y_recv.at[src_e, :, pl.ds(first, count)],
-            send_sem=y_send_sem.at[src_e, first // piece],
-            recv_sem=y_recv_sem.at[src_e, first // piece],
+            send_sem=y_send_sem.at[src_e, index],
+            recv_sem=y_recv_sem.at[src_e, index],
             device_id=(c, partner),
             device_id_type=MESH,
         )
@@ -250,33 +251,18 @@
     slot_gate[...] = jnp.sum(chosen * gate, axis=1, keepdims=True)[:cap]
     gate_acc[...] = jnp.zeros_like(gate_acc)
 
-    def dexp_copy(src, part):
-        first, count = part
-        cols = pl.ds(pl.multiple_of(src * width + first, HD), count)
-        return pltpu.make_async_copy(
-            dexp_out.at[:, cols], dexp_hbm.at[0, :, cols], dexp_sem.at[src, first // piece]
-        )
-
-    out_copies = [
-        pltpu.make_async_copy(source, target, out_sem.at[i])
-        for i, (source, target) in enumerate(
-            ((dq_out, dq_hbm), (dk_out, dk_hbm), (dv_out, dv_hbm), (dgate_out, dgate_hbm))
-        )
-    ]
-
     def finish(src, part, routed):
-        first, count = part
+        first, count, _ = part
         cols = pl.ds(pl.multiple_of(src * width + first, HD), count)
         product = routed * eo[:, cols].astype(F32)
         total = gate_acc[...]
         for i in range(count // HD):
             total += product[:, i * HD : (i + 1) * HD]
         gate_acc[...] = total
-        dexp_out[:, cols] = (slot_gate[...] * routed).astype(BF16)
-        dexp_copy(src, part).start()
+        dexp_out[0, :, cols] = (slot_gate[...] * routed).astype(BF16)
 
     def take(src_e, part):
-        first, count = part
+        first, count, index = part
         cols = pl.ds(first, count)
         picked = dot(pick[...], rows[src_e, :, cols], ((1,), (0,)))
         y_send[src_e, :, cols] = picked[cap:].astype(BF16)
@@ -284,7 +270,7 @@
         finish(src_e * 2 + y, part, picked[:cap])
 
     def take_other(src_e, part):
-        first, count = part
+        first, count, index = part
         y_copy(src_e, part).wait_recv()
         other = y_recv[src_e, :, pl.ds(first, count)]
         finish(src_e * 2 + 1 - y, part, other.astype(F32))
@@ -406,7 +392,6 @@
     part_copy(0, 1).start()
     for h in range(QH_DEV):
         dq_out[:, h * HD : (h + 1) * HD] = (dq_acc[h * n : (h + 1) * n] * scaling).astype(BF16)
-    out_copies[0].start()
 
     def arrive(step):
         for part in parts_at(step):
@@ -415,7 +400,7 @@
                 @pl.when(jnp.logical_and(present, jnp.logical_not(passes(way))))
                 def _():
                     for k in range(chunks):
-                        if part[0] <= k * piece < part[0] + part[1]:
+                        if part[0] <= pieces[k][0] < part[0] + part[1]:
                             row_copy(way, src_e, k).wait_recv()
 
                 @pl.when(present)
@@ -449,8 +434,6 @@
         summed = part_own[...].T.astype(BF16)
         dk_out[...] = summed[: HD // 2]
         dv_out[...] = summed[HD // 2 :]
-        out_copies[1].start()
-        out_copies[2].start()
 
     for step in range(1, experts):
         forward(step + 1, 0)
@@ -464,11 +447,8 @@
 
     gate_sum = jnp.sum(gate_acc[...], axis=1, keepdims=True)
     dgate_out[...] = jnp.broadcast_to(gate_sum, (cap, HD)).T[:1]
-    out_copies[3].start()
 
     y_copy(e, whole[0]).wait_send()
-    dexp_copy(e * 2, whole[0]).wait()
-    dexp_copy(e * 2 + 1, whole[0]).wait()
     for k in range(chunks):
 
         @pl.when(e < experts - 1)
@@ -486,16 +466,12 @@
             def _():
                 for part in parts_at(step):
                     y_copy(src_e, part).wait_send()
-                    dexp_copy(src_e * 2, part).wait()
-                    dexp_copy(src_e * 2 + 1, part).wait()
 
                 @pl.when(e < experts - 1 if way == 0 else e > 0)
                 def _():
                     for k in range(chunks):
                         row_copy(way, src_e, k).wait_send()
 
-    for copy in out_copies:
-        copy.wait()
     part_copy(0, 1).wait_send()
     for o in range(1, reach + 1):
 
@@ -510,27 +486,14 @@
 
 
 def write(*refs):
-    sources, targets, held, sem = refs[:5], refs[5:10], refs[10:15], refs[15]
-    into, out = [], []
-
-    def through(source, hold, target):
-        i = len(into)
-        into.append(pltpu.make_async_copy(source, hold, sem.at[0, i]))
-        out.append(pltpu.make_async_copy(hold, target, sem.at[1, i]))
-
-    for source, target, hold in zip(sources, targets, held):
-        if len(source.shape) == 2:
-            through(source, hold, target)
-            continue
-        for row in range(0, source.shape[1], 16):
-            at = pl.ds(row, 16)
-            through(source.at[0, at], hold.at[0, at], target.at[0, at])
-    for copy in into:
+    sources, targets, sem = refs[:5], refs[5:10], refs[10]
+    copies = [
+        pltpu.make_async_copy(source, target, sem.at[i])
+        for i, (source, target) in enumerate(zip(sources, targets))
+    ]
+    for copy in reversed(copies):
         copy.start()
-    for first, second in zip(into, out):
-        first.wait()
-        second.start()
-    for copy in out:
+    for copy in copies:
         copy.wait()
 
 
@@ -551,7 +514,7 @@
     cap, features = expert_out.shape[1:]
     experts = tp_size // 2
     reach = min((doc_ids.shape[0] // 2 + n) // n, ctx_size - 1)
-    chunks = 2 if width % (2 * HD) == 0 else 1
+    chunks = len(cuts(width))
     blocks = reach + 1
     stacked = QH_DEV * n
     dma = pltpu.SemaphoreType.DMA
@@ -563,13 +526,11 @@
         jax.ShapeDtypeStruct(expert_out.shape, BF16),
     )
     outs = pl.pallas_call(
-        functools.partial(kernel, ctx_size, tp_size, reach, chunks),
-        out_shape=out_shape,
+        functools.partial(kernel, ctx_size, tp_size, reach),
+        out_shape=tuple(pltpu.VMEM(out.shape, out.dtype) for out in out_shape),
         in_specs=[pl.BlockSpec(memory_space=pltpu.HBM)] * 10,
-        out_specs=[pl.BlockSpec(memory_space=pltpu.HBM)] * 5,
+        out_specs=[pl.BlockSpec(memory_space=pltpu.VMEM)] * 5,
         scratch_shapes=[
-            *(pltpu.VMEM(out.shape, out.dtype) for out in out_shape[:4]),
-            pltpu.VMEM((cap, features), BF16),
             pltpu.VMEM(queries.shape, BF16),
             pltpu.VMEM(queries.shape, BF16),
             pltpu.VMEM(queries.shape, BF16),
@@ -606,35 +567,34 @@
             dma((experts, chunks)),
             dma((experts, chunks)),
             dma((experts, chunks)),
-            dma((4,)),
-            dma((tp_size, chunks)),
         ],
         compiler_params=pltpu.CompilerParams(
             collective_id=0, has_side_effects=True, vmem_limit_bytes=VMEM
         ),
         name="backward",
     )(
-        queries,
-        key_rows,
-        value_rows,
-        out_grad,
-        attn_out,
-        doc_ids.reshape(-1, n),
-        row_grad,
-        gate_weights.T,
-        expert_ids.T,
-        expert_out,
+        *(
+            pltpu.with_memory_space_constraint(operand, pltpu.HBM)
+            for operand in (
+                queries,
+                key_rows,
+                value_rows,
+                out_grad,
+                attn_out,
+                doc_ids.reshape(-1, n),
+                row_grad,
+                gate_weights.T,
+                expert_ids.T,
+                expert_out,
+            )
+        )
     )
     query_grad, key_grad, value_grad, gate_grad, expert_grad = pl.pallas_call(
         write,
         out_shape=out_shape,
-        in_specs=[pl.BlockSpec(memory_space=pltpu.HBM)] * 5,
+        in_specs=[pl.BlockSpec(memory_space=pltpu.VMEM)] * 5,
         out_specs=[pl.BlockSpec(memory_space=pltpu.HBM)] * 5,
-        scratch_shapes=[
-            *(pltpu.VMEM(out.shape, out.dtype) for out in out_shape),
-            dma((2, 4 + cap // 16)),
-        ],
-        compiler_params=pltpu.CompilerParams(vmem_limit_bytes=VMEM),
+        scratch_shapes=[dma((5,))],
         name="write",
     )(*outs)
     return (query_grad, key_grad.T, value_grad.T, gate_grad, expert_grad)

time: 27.7 us -> 29.2 us (1.054)
  local copies, waits for them, and re-layouts: 0 us -> 3.33 us
  Pallas kernels: 26.9 us -> 25.1 us
    unnamed x0 -> x10, local copies, waits for them, and re-layouts: none -> 3.33 us
    pallas_call x1, Pallas kernels: 24.8 us -> 22.9 us  [local(): pl.pallas_call(functools.partial(kernel, ctx_size, tp_size, reach), out_s...]
where the time goes in v5:
time: 29.2 us; the launch traced here: 29.1 us
  Pallas kernels  25.1 us (86%)
  local copies, waits for them, and re-layouts  3.33 us (11%)
  between operations  0.66 us (2%)
    pallas_call x1, Pallas kernels, local(): pl.pallas_call(functools.partial(kernel, ctx_size, tp_size, reach), out_s...  22.9 us
    unnamed x10, local copies, waits for them, and re-layouts  3.33 us
    pallas_call x1, Pallas kernels, local(): pl.pallas_call(write, out_shape=out_shape, in_specs=[pl.BlockSpec(memory_...  2.19 us

profile of v5, /device:TPU:0, one launch (start us, length us, event | category | flops | bytes accessed | tf_op | source)
XLA Modules:
  0.0 29.1 jit_solution(9974476413821542689)
XLA Ops:
  0.6 22.9 %backward.1 = (bf16[128,384]{1,0:T(8,128)(2,1)S(1)}, bf16[64,128]{1,0:T(8,128)(2,1)S(1)}, bf16[64,128]{1,0:T(8,128)(2,1)S(1)}, f32[1,64]{1,0:T(1,128)S(1)}, bf16[1,64,6144]{2,1,0:T(8,128)(2,1)S(1)}) custom-call(bf16[128,384]{1,0:T(8,128)(2,1)} %q_in.1, bf16[128,512]{1,0:T(8,128)(2,1)} %k_in.1, bf16[128,512]{1,0:T(8,128)(2,1)} %v_in.1, ...), custom_call_target="tpu_custom_call" | custom-call | tf_op jit(solution)/shard_map/backward/pallas_call | solution.py:528
  23.5 0.0 copy-start
  23.6 0.9 %copy-done = bf16[1,64,6144]{2,1,0:T(8,128)(2,1)} copy-done((bf16[1,64,6144]{2,1,0:T(8,128)(2,1)}, bf16[1,64,6144]{2,1,0:T(8,128)(2,1)S(1)}, u32[]{:S(2)}) %copy-start) | copy-done | bytes 786456
  24.4 0.0 copy-start.1
  24.4 0.6 %copy-done.1 = bf16[128,384]{1,0:T(8,128)(2,1)} copy-done((bf16[128,384]{1,0:T(8,128)(2,1)}, bf16[128,384]{1,0:T(8,128)(2,1)S(1)}, u32[]{:S(2)}) %copy-start.1) | copy-done | bytes 98328
  25.1 0.0 copy-start.2
  25.1 0.6 %copy-done.2 = bf16[64,128]{1,0:T(8,128)(2,1)} copy-done((bf16[64,128]{1,0:T(8,128)(2,1)}, bf16[64,128]{1,0:T(8,128)(2,1)S(1)}, u32[]{:S(2)}) %copy-start.2) | copy-done | bytes 16408
  25.7 0.0 copy-start.3
  25.7 0.6 %copy-done.3 = bf16[64,128]{1,0:T(8,128)(2,1)} copy-done((bf16[64,128]{1,0:T(8,128)(2,1)}, bf16[64,128]{1,0:T(8,128)(2,1)S(1)}, u32[]{:S(2)}) %copy-start.3) | copy-done | bytes 16408
  26.3 0.0 copy-start.4
  26.3 0.6 %copy-done.4 = f32[1,64]{1,0:T(1,128)} copy-done((f32[1,64]{1,0:T(1,128)}, f32[1,64]{1,0:T(1,128)S(1)}, u32[]{:S(2)}) %copy-start.4) | copy-done | bytes 280
  26.9 2.2 %write.1 = (bf16[128,384]{1,0:T(8,128)(2,1)}, bf16[64,128]{1,0:T(8,128)(2,1)}, bf16[64,128]{1,0:T(8,128)(2,1)}, f32[1,64]{1,0:T(1,128)}, bf16[1,64,6144]{2,1,0:T(8,128)(2,1)}) custom-call(bf16[128,384]{1,0:T(8,128)(2,1)} %copy-done.1, bf16[64,128]{1,0:T(8,128)(2,1)} %copy-done.2, bf16[64,128]{1,0:T(8,128)(2,1)} %copy-done.3, f32[1,64]{1,0:T(1,128)} %copy-done.4, ...), custom_call_target="tpu_custom_call" | custom-call | tf_op jit(solution)/shard_map/write/pallas_call | solution.py:592
Async XLA Ops:
  23.5 0.9 %copy-start = (bf16[1,64,6144]{2,1,0:T(8,128)(2,1)}, bf16[1,64,6144]{2,1,0:T(8,128)(2,1)S(1)}, u32[]{:S(2)}) copy-start(bf16[1,64,6144]{2,1,0:T(8,128)(2,1)S(1)} %get-tuple-element.19.refs_4_) | copy-start | bytes 2359300
  24.4 0.6 %copy-start.1 = (bf16[128,384]{1,0:T(8,128)(2,1)}, bf16[128,384]{1,0:T(8,128)(2,1)S(1)}, u32[]{:S(2)}) copy-start(bf16[128,384]{1,0:T(8,128)(2,1)S(1)} %get-tuple-element.15.refs_0_) | copy-start | bytes 294916
  25.1 0.6 %copy-start.2 = (bf16[64,128]{1,0:T(8,128)(2,1)}, bf16[64,128]{1,0:T(8,128)(2,1)S(1)}, u32[]{:S(2)}) copy-start(bf16[64,128]{1,0:T(8,128)(2,1)S(1)} %get-tuple-element.16.refs_1_) | copy-start | bytes 49156
  25.7 0.6 %copy-start.3 = (bf16[64,128]{1,0:T(8,128)(2,1)}, bf16[64,128]{1,0:T(8,128)(2,1)S(1)}, u32[]{:S(2)}) copy-start(bf16[64,128]{1,0:T(8,128)(2,1)S(1)} %get-tuple-element.17.refs_2_) | copy-start | bytes 49156
  26.3 0.6 %copy-start.4 = (f32[1,64]{1,0:T(1,128)}, f32[1,64]{1,0:T(1,128)S(1)}, u32[]{:S(2)}) copy-start(f32[1,64]{1,0:T(1,128)S(1)} %get-tuple-element.18.refs_3_) | copy-start | bytes 772

commit v6 on v5

--- a/solution.py
+++ b/solution.py
@@ -595,6 +595,7 @@
         in_specs=[pl.BlockSpec(memory_space=pltpu.VMEM)] * 5,
         out_specs=[pl.BlockSpec(memory_space=pltpu.HBM)] * 5,
         scratch_shapes=[dma((5,))],
+        compiler_params=pltpu.CompilerParams(vmem_limit_bytes=8 * 1024 * 1024),
         name="write",
     )(*outs)
     return (query_grad, key_grad.T, value_grad.T, gate_grad, expert_grad)

time: 29.2 us -> 24.7 us (0.85)
  local copies, waits for them, and re-layouts: 3.33 us -> 0 us
  Pallas kernels: 25.1 us -> 23.9 us
    unnamed x10 -> x0, local copies, waits for them, and re-layouts: 3.33 us -> none
    pallas_call x1, Pallas kernels: 2.19 us -> 0.97 us  [local(): pl.pallas_call(write, out_shape=out_shape, in_specs=[pl.BlockSpec(memory_...]
where the time goes in v6:
time: 24.7 us; the launch traced here: 24.5 us
  Pallas kernels  23.9 us (97%)
  between operations  0.64 us (3%)
    pallas_call x1, Pallas kernels, local(): pl.pallas_call(functools.partial(kernel, ctx_size, tp_size, reach), out_s...  22.9 us
    pallas_call x1, Pallas kernels, local(): pl.pallas_call(write, out_shape=out_shape, in_specs=[pl.BlockSpec(memory_...  0.97 us

profile of v6, /device:TPU:0, one launch (start us, length us, event | category | flops | bytes accessed | tf_op | source)
XLA Modules:
  0.0 24.5 jit_solution(1779559424401041244)
XLA Ops:
  0.6 22.9 %backward.1 = (bf16[128,384]{1,0:T(8,128)(2,1)S(1)}, bf16[64,128]{1,0:T(8,128)(2,1)S(1)}, bf16[64,128]{1,0:T(8,128)(2,1)S(1)}, f32[1,64]{1,0:T(1,128)S(1)}, bf16[1,64,6144]{2,1,0:T(8,128)(2,1)S(1)}) custom-call(bf16[128,384]{1,0:T(8,128)(2,1)} %q_in.1, bf16[128,512]{1,0:T(8,128)(2,1)} %k_in.1, bf16[128,512]{1,0:T(8,128)(2,1)} %v_in.1, ...), custom_call_target="tpu_custom_call" | custom-call | tf_op jit(solution)/shard_map/backward/pallas_call | solution.py:528
  23.5 1.0 %write.1 = (bf16[128,384]{1,0:T(8,128)(2,1)}, bf16[64,128]{1,0:T(8,128)(2,1)}, bf16[64,128]{1,0:T(8,128)(2,1)}, f32[1,64]{1,0:T(1,128)}, bf16[1,64,6144]{2,1,0:T(8,128)(2,1)}) custom-call(bf16[128,384]{1,0:T(8,128)(2,1)S(1)} %get-tuple-element.15.refs_0_, bf16[64,128]{1,0:T(8,128)(2,1)S(1)} %get-tuple-element.16.refs_1_, ...), custom_call_target="tpu_custom_call" | custom-call | tf_op jit(solution)/shard_map/write/pallas_call | solution.py:592

commit v7 on v6

--- a/solution.py
+++ b/solution.py
@@ -168,7 +168,7 @@
     pl.semaphore_wait(barrier, greeted)
 
     def row_copy(way, src_e, k):
-        to = t + 2 if way == 0 else t - 2
+        to = jnp.minimum(t + 2, tp_size - 1) if way == 0 else jnp.maximum(t - 2, 0)
         return pltpu.make_async_remote_copy(
             src_ref=rows.at[src_e, :, cut(k)],
             dst_ref=rows.at[src_e, :, cut(k)],
@@ -200,7 +200,7 @@
             dst_ref=kv.at[o],
             send_sem=kv_send_sem.at[o],
             recv_sem=kv_recv_sem.at[o],
-            device_id=(c + o, t),
+            device_id=(jnp.minimum(c + o, ctx_size - 1), t),
             device_id_type=MESH,
         )
 
@@ -210,7 +210,7 @@
             dst_ref=part_recv.at[o, which],
             send_sem=part_send_sem.at[o, which],
             recv_sem=part_recv_sem.at[o, which],
-            device_id=(c - o, t if which == 0 else partner),
+            device_id=(jnp.maximum(c - o, 0), t if which == 0 else partner),
             device_id_type=MESH,
         )
 
@@ -315,7 +315,24 @@
         def _():
             kv[o] = jnp.zeros(kv.shape[1:], BF16)
 
+    def forward(step, k):
+        if step >= experts:
+            return
+        for way, src_e, present in sources(step):
+
+            @pl.when(jnp.logical_and(present, passes(way)))
+            def _():
+                row_copy(way, src_e, k).wait_recv()
+                row_copy(way, src_e, k).start()
+
+    def passes(way):
+        return e < experts - 1 if way == 0 else e > 0
+
+    def sources(step):
+        return ((0, e - step, e >= step), (1, e + step, e + step < experts))
+
     each(reach + 1, scores_of)
+    forward(1, 0)
     row_max = jnp.max(score_max[...], axis=1, keepdims=True)
     score_max[...] = jnp.broadcast_to(row_max, score_max.shape)
 
@@ -349,26 +366,9 @@
             part_copy(o, 0).start()
             part_copy(o, 1).start()
 
-    def forward(step, k):
-        if step >= experts:
-            return
-        for way, src_e, present in sources(step):
-
-            @pl.when(jnp.logical_and(present, passes(way)))
-            def _():
-                row_copy(way, src_e, k).wait_recv()
-                row_copy(way, src_e, k).start()
-
-    def passes(way):
-        return e < experts - 1 if way == 0 else e > 0
-
-    def sources(step):
-        return ((0, e - step, e >= step), (1, e + step, e + step < experts))
-
     if reach <= 3:
         late = list(range(reach, reach // 2, -1))
         near = list(range(reach // 2, -1, -1))
-        forward(1, 0)
         for o in late:
             grads_of(o)
         for o in late:
@@ -380,7 +380,7 @@
         for o in near[:-1]:
             send_parts(o)
     else:
-        for k in range(chunks):
+        for k in range(1, chunks):
             forward(1, k)
 
         @pl.loop(0, reach)

time: 24.7 us -> 24.7 us (level)
  no operation moved by 1% of the time
where the time goes in v7:
time: 24.7 us; the launch traced here: 24.5 us
  Pallas kernels  23.9 us (97%)
  between operations  0.64 us (3%)
    pallas_call x1, Pallas kernels, local(): pl.pallas_call(functools.partial(kernel, ctx_size, tp_size, reach), out_s...  22.9 us
    pallas_call x1, Pallas kernels, local(): pl.pallas_call(write, out_shape=out_shape, in_specs=[pl.BlockSpec(memory_...  0.97 us

profile of v7, /device:TPU:0, one launch (start us, length us, event | category | flops | bytes accessed | tf_op | source)
XLA Modules:
  0.0 24.5 jit_solution(14115469309111302758)
XLA Ops:
  0.6 22.9 %backward.1 = (bf16[128,384]{1,0:T(8,128)(2,1)S(1)}, bf16[64,128]{1,0:T(8,128)(2,1)S(1)}, bf16[64,128]{1,0:T(8,128)(2,1)S(1)}, f32[1,64]{1,0:T(1,128)S(1)}, bf16[1,64,6144]{2,1,0:T(8,128)(2,1)S(1)}) custom-call(bf16[128,384]{1,0:T(8,128)(2,1)} %q_in.1, bf16[128,512]{1,0:T(8,128)(2,1)} %k_in.1, bf16[128,512]{1,0:T(8,128)(2,1)} %v_in.1, ...), custom_call_target="tpu_custom_call" | custom-call | tf_op jit(solution)/shard_map/backward/pallas_call | solution.py:528
  23.6 1.0 %write.1 = (bf16[128,384]{1,0:T(8,128)(2,1)}, bf16[64,128]{1,0:T(8,128)(2,1)}, bf16[64,128]{1,0:T(8,128)(2,1)}, f32[1,64]{1,0:T(1,128)}, bf16[1,64,6144]{2,1,0:T(8,128)(2,1)}) custom-call(bf16[128,384]{1,0:T(8,128)(2,1)S(1)} %get-tuple-element.15.refs_0_, bf16[64,128]{1,0:T(8,128)(2,1)S(1)} %get-tuple-element.16.refs_1_, ...), custom_call_target="tpu_custom_call" | custom-call | tf_op jit(solution)/shard_map/write/pallas_call | solution.py:592
